TPU v7x, 768 devices: a whole 4x8x12 slice. The times are simulated.
768 devices in a mesh: lon: 96 (over z, y_hi, x), lat: 8 (over y_lo, core).
Axes of the slice: x: 4, y: 8 (y_hi: 2, y_lo: 4; y = y_hi * 4 + y_lo), z: 12, core: 2. Of those that a mesh axis runs over, the one named last changes fastest.
Arguments:
- right_side: float32 [70, 384, 1024], P(None, 'lon', 'lat'), may hold values from -12 to 12
- first_guess: float32 [70, 384, 1024], P(None, 'lon', 'lat'), may hold values from -1.8 to 1.8
- cell_scale: float32 [70, 384, 1024], P(None, 'lon', 'lat'), may hold values from 0.6 to 1.6
- helmholtz_term: float32 [70, 384, 1024], P(None, 'lon', 'lat'), may hold values from 0.05 to 0.5
- vertical_coupling: float32 [69], replicated, may hold values from 0.5 to 4
Outputs:
- solution: float32 [70, 384, 1024], P(None, 'lon', 'lat')
- residual: float32 [70, 384, 1024], P(None, 'lon', 'lat')
All inputs are finite; a program needn't handle non-finite values.
Results may differ from a plain program's by a relative error of at most 0.00026.
Values sent between devices are 32-bit elements; how exact they have to be, the bound alone decides.
A program may use at most 32 MiB of HBM per device.

v0:
```python
import jax
import jax.numpy as jnp
from jax import lax
from jax.sharding import PartitionSpec as P

ITERS = 2


def padded(value, sides, width, wrap):
    for axis, dim in sides:
        peers, length = (lax.axis_size(axis), value.shape[dim])
        up = [(i, (i + 1) % peers) for i in range(peers if wrap else peers - 1)]
        down = [(j, i) for i, j in up]
        last = lax.slice_in_dim(value, length - width, length, axis=dim)
        leading = lax.slice_in_dim(value, 0, width, axis=dim)
        before = lax.ppermute(last, axis, up)
        after = lax.ppermute(leading, axis, down)
        value = jnp.concatenate([before, value, after], axis=dim)
    return value


def shifted(value, axis, steps):
    count = lax.axis_size(axis)
    pairs = [(source, (source + steps) % count) for source in range(count)]
    return lax.ppermute(value, axis, pairs)


def extend(stacked):
    lon_side = padded(stacked, (("lon", 2),), 1, True)
    lat_side = padded(stacked, (("lat", 3),), 1, False)
    edge_rows = jnp.concatenate([stacked[..., :1], stacked[..., -1:]], axis=3)
    partner = shifted(edge_rows, "lon", lax.axis_size("lon") // 2)
    band_index = lax.axis_index("lat")
    last_band = lax.axis_size("lat") - 1
    top_row = jnp.where(band_index == 0, partner[..., :1], lat_side[..., :1])
    bottom = jnp.where(band_index == last_band, partner[..., 1:], lat_side[..., -1:])
    lat_side = jnp.concatenate([top_row, lat_side[..., 1:-1], bottom], axis=3)
    return (lon_side, lat_side)


def reduce_all(terms):
    return lax.psum(terms, ("lon", "lat"))


def apply_operator(
    field, lon_side, lat_side, cell_scale, scale_lon, scale_lat, helmholtz_term, vertical_coupling
):
    scaled = cell_scale * field
    scaled_lon = scale_lon * lon_side
    scaled_lat = scale_lat * lat_side
    horizontal = (
        (4.0 + helmholtz_term) * scaled
        - scaled_lon[:, 2:, :]
        - scaled_lon[:, :-2, :]
        - scaled_lat[:, :, :-2]
        - scaled_lat[:, :, 2:]
    )
    vert_flux = vertical_coupling[:, None, None] * (scaled[:-1] - scaled[1:])
    zero_layer = jnp.zeros_like(scaled[:1])
    vertical = jnp.concatenate([vert_flux, zero_layer], axis=0) - jnp.concatenate(
        [zero_layer, vert_flux], axis=0
    )
    return cell_scale * (horizontal + vertical)


def body(right_side, first_guess, cell_scale, helmholtz_term, vertical_coupling):
    start_lon, start_lat = extend(jnp.stack([cell_scale, first_guess]))
    scale_lon = start_lon[0]
    scale_lat = start_lat[0]

    def operate(field, lon_side, lat_side):
        return apply_operator(
            field,
            lon_side,
            lat_side,
            cell_scale,
            scale_lon,
            scale_lat,
            helmholtz_term,
            vertical_coupling,
        )

    solution = first_guess
    residual = right_side - operate(first_guess, start_lon[1], start_lat[1])
    shadow = residual
    direction = residual
    rho_now = None
    for iteration in range(ITERS):
        dir_lon, dir_lat = extend(direction[None])
        image_vec = operate(direction, dir_lon[0], dir_lat[0])
        if iteration == 0:
            rho_now, denominator = reduce_all(
                (jnp.sum(residual * residual), jnp.sum(shadow * image_vec))
            )
        else:
            (denominator,) = reduce_all((jnp.sum(shadow * image_vec),))
        alpha_step = rho_now / denominator
        half_step = residual - alpha_step * image_vec
        half_lon, half_lat = extend(half_step[None])
        half_lon = half_lon[0]
        half_lat = half_lat[0]
        second_image = operate(half_step, half_lon, half_lat)
        if iteration + 1 < ITERS:
            tee_half, tee_tee, shadow_half, shadow_tee = reduce_all(
                (
                    jnp.sum(second_image * half_step),
                    jnp.sum(second_image * second_image),
                    jnp.sum(shadow * half_step),
                    jnp.sum(shadow * second_image),
                )
            )
        else:
            tee_half, tee_tee = reduce_all(
                (jnp.sum(second_image * half_step), jnp.sum(second_image * second_image))
            )
        omega_step = tee_half / tee_tee
        solution = solution + alpha_step * direction + omega_step * half_step
        residual = half_step - omega_step * second_image
        if iteration + 1 < ITERS:
            rho_next = shadow_half - omega_step * shadow_tee
            beta_step = rho_next / rho_now * (alpha_step / omega_step)
            direction = residual + beta_step * (direction - omega_step * image_vec)
            rho_now = rho_next
    return (solution, residual)


def solution(mesh):
    in_specs = (
        P(None, "lon", "lat"),
        P(None, "lon", "lat"),
        P(None, "lon", "lat"),
        P(None, "lon", "lat"),
        P(),
    )
    out_specs = (P(None, "lon", "lat"), P(None, "lon", "lat"))
    return jax.shard_map(body, mesh=mesh, in_specs=in_specs, out_specs=out_specs, check_vma=False)
```

profile of v0, /device:TPU:1, one launch (start us, length us, event | category | flops | bytes accessed | tf_op | source)
XLA Modules:
  0.0 597.3 jit_solution(13370236572273237130)
XLA Ops:
  1.9 4.6 collective-permute-start.3
  6.5 9.1 %collective-permute-start.4 = (f32[2,70,4,1]{1,3,2,0:T(1,128)S(1)}, f32[2,70,4,1]{1,3,2,0:T(1,128)S(1)}, u32[]{:S(2)}, u32[]{:S(2)}) collective-permute-start(f32[2,70,4,1]{1,3,2,0:T(1,128)S(1)} %get-tuple-element.40), channel_id=1, source_target_pairs={{1,0},{2,1},{3,2},{4,3},{5,4},{6,5},{7,6},{9,8},{10,9},{11,10},{12... | collective-permute-start | bytes 6728 | tf_op jit(solution)/shard_map/ppermute | solution.py:17
  15.6 7.7 %collective-permute-start.2 = (f32[2,70,4,2]{1,3,2,0:T(2,128)S(1)}, f32[2,70,4,2]{1,3,2,0:T(2,128)S(1)}, u32[]{:S(2)}, u32[]{:S(2)}) collective-permute-start(f32[2,70,4,2]{1,3,2,0:T(2,128)S(1)} %pad_maximum_fusion.2), channel_id=1, source_target_pairs={{0,384},{8,392},{16,400},{24,408},{32,416},{40,424},{48,432},{56,4... | collective-permute-start | bytes 13448 | tf_op jit(solution)/shard_map/ppermute | solution.py:25
  23.3 3.1 collective-permute-start
  26.5 10.3 %collective-permute-start.1 = (f32[2,70,1,128]{1,3,2,0:T(8,128)S(1)}, f32[2,70,1,128]{1,3,2,0:T(8,128)S(1)}, u32[]{:S(2)}, u32[]{:S(2)}) collective-permute-start(f32[2,70,1,128]{1,3,2,0:T(8,128)S(1)} %get-tuple-element.38), channel_id=1, source_target_pairs={{8,0},{16,8},{24,16},{32,24},{40,32},{48,40},{56,48},{64,56},{72,6... | collective-permute-start | bytes 215048 | tf_op jit(solution)/shard_map/ppermute | solution.py:17
  40.0 4.1 collective-permute-start.8
  44.1 1.9 collective-permute-start.9
  46.1 6.0 collective-permute-start.7
  53.9 12.8 %collective-permute-start.6 = (f32[1,70,1,128]{1,3,2,0:T(8,128)S(1)}, f32[1,70,1,128]{1,3,2,0:T(8,128)S(1)}, u32[]{:S(2)}, u32[]{:S(2)}) collective-permute-start(f32[1,70,1,128]{1,3,2,0:T(8,128)S(1)} %get-tuple-element.56), channel_id=1, source_target_pairs={{8,0},{16,8},{24,16},{32,24},{40,32},{48,40},{56,48},{64,56},{72,6... | collective-permute-start | bytes 107528 | tf_op jit(solution)/shard_map/ppermute | solution.py:17
  68.9 111.2 %all-reduce.12 = (f32[]{:T(128)}, f32[]{:T(128)}) all-reduce(f32[]{:T(128)} %get-tuple-element.15, f32[]{:T(128)} %get-tuple-element.14), channel_id=1, replica_groups=mesh['lon'=96,'lat'=8] {'lon','lat'}, use_global_device_ids=true, to_apply=%region_1.2 | all-reduce | flops 2 | bytes 16 | tf_op jit(solution)/shard_map/psum | solution.py:42
  183.5 2.4 collective-permute-start.14
  185.9 4.9 collective-permute-start.12
  192.7 11.5 %collective-permute-start.11 = (f32[1,70,1,128]{1,3,2,0:T(8,128)S(1)}, f32[1,70,1,128]{1,3,2,0:T(8,128)S(1)}, u32[]{:S(2)}, u32[]{:S(2)}) collective-permute-start(f32[1,70,1,128]{1,3,2,0:T(8,128)S(1)} %get-tuple-element.52), channel_id=1, source_target_pairs={{8,0},{16,8},{24,16},{32,24},{40,32},{48,40},{56,48},{64,56},{72,6... | collective-permute-start | bytes 107528 | tf_op jit(solution)/shard_map/ppermute | solution.py:17
  206.8 108.5 %all-reduce.11 = (f32[]{:T(128)}, f32[]{:T(128)}, f32[]{:T(128)}, f32[]{:T(128)}) all-reduce(f32[]{:T(128)} %get-tuple-element.13, f32[]{:T(128)} %get-tuple-element.12, f32[]{:T(128)} %get-tuple-element.11, f32[]{:T(128)} %get-tuple-element.10), channel_id=1, replica_groups=mesh['lon'=96,'lat'=8] {'lon','lat'}, use_global_device_ids=true, to_apply=%region_9.10 | all-reduce | flops 4 | bytes 32 | tf_op jit(solution)/shard_map/psum | solution.py:42
  323.2 2.4 collective-permute-start.19
  325.6 5.5 collective-permute-start.17
  331.1 1.9 collective-permute-start.15
  333.0 11.5 %collective-permute-start.16 = (f32[1,70,1,128]{1,3,2,0:T(8,128)S(1)}, f32[1,70,1,128]{1,3,2,0:T(8,128)S(1)}, u32[]{:S(2)}, u32[]{:S(2)}) collective-permute-start(f32[1,70,1,128]{1,3,2,0:T(8,128)S(1)} %get-tuple-element.48), channel_id=1, source_target_pairs={{8,0},{16,8},{24,16},{32,24},{40,32},{48,40},{56,48},{64,56},{72,6... | collective-permute-start | bytes 107528 | tf_op jit(solution)/shard_map/ppermute | solution.py:17
  347.6 111.9 %psum.69 = f32[]{:T(128)} all-reduce(f32[]{:T(128)} %get-tuple-element.27), channel_id=1, replica_groups=mesh['lon'=96,'lat'=8] {'lon','lat'}, use_global_device_ids=true, to_apply=%region_13.14 | all-reduce | flops 1 | bytes 8 | tf_op jit(solution)/shard_map/psum | solution.py:42
  463.1 2.4 collective-permute-start.24
  465.5 4.3 collective-permute-start.22
  469.8 1.9 collective-permute-start.20
  471.8 11.5 %collective-permute-start.21 = (f32[1,70,1,128]{1,3,2,0:T(8,128)S(1)}, f32[1,70,1,128]{1,3,2,0:T(8,128)S(1)}, u32[]{:S(2)}, u32[]{:S(2)}) collective-permute-start(f32[1,70,1,128]{1,3,2,0:T(8,128)S(1)} %get-tuple-element.44), channel_id=1, source_target_pairs={{8,0},{16,8},{24,16},{32,24},{40,32},{48,40},{56,48},{64,56},{72,6... | collective-permute-start | bytes 107528 | tf_op jit(solution)/shard_map/ppermute | solution.py:17
  485.7 108.6 %all-reduce.10 = (f32[]{:T(128)}, f32[]{:T(128)}) all-reduce(f32[]{:T(128)} %get-tuple-element.9, f32[]{:T(128)} %get-tuple-element.8), channel_id=1, replica_groups=mesh['lon'=96,'lat'=8] {'lon','lat'}, use_global_device_ids=true, to_apply=%region_15.16 | all-reduce | flops 2 | bytes 16 | tf_op jit(solution)/shard_map/psum | solution.py:42
  (91 shorter events, 26.9 us)
Async XLA Ops:
  1.9 36.9 %collective-permute-start.3 = (f32[2,70,4,1]{1,3,2,0:T(1,128)S(1)}, f32[2,70,4,1]{1,3,2,0:T(1,128)S(1)}, u32[]{:S(2)}, u32[]{:S(2)}) collective-permute-start(f32[2,70,4,1]{1,3,2,0:T(1,128)S(1)} %get-tuple-element.39), channel_id=1, source_target_pairs={{0,1},{1,2},{2,3},{3,4},{4,5},{5,6},{6,7},{8,9},{9,10},{10,11},{11... | collective-permute-start | bytes 6728 | tf_op jit(solution)/shard_map/ppermute | solution.py:16
  6.5 32.3 %collective-permute-start.4 = (f32[2,70,4,1]{1,3,2,0:T(1,128)S(1)}, f32[2,70,4,1]{1,3,2,0:T(1,128)S(1)}, u32[]{:S(2)}, u32[]{:S(2)}) collective-permute-start(f32[2,70,4,1]{1,3,2,0:T(1,128)S(1)} %get-tuple-element.40), channel_id=1, source_target_pairs={{1,0},{2,1},{3,2},{4,3},{5,4},{6,5},{7,6},{9,8},{10,9},{11,10},{12... | collective-permute-start | bytes 6728 | tf_op jit(solution)/shard_map/ppermute | solution.py:17
  15.6 23.2 %collective-permute-start.2 = (f32[2,70,4,2]{1,3,2,0:T(2,128)S(1)}, f32[2,70,4,2]{1,3,2,0:T(2,128)S(1)}, u32[]{:S(2)}, u32[]{:S(2)}) collective-permute-start(f32[2,70,4,2]{1,3,2,0:T(2,128)S(1)} %pad_maximum_fusion.2), channel_id=1, source_target_pairs={{0,384},{8,392},{16,400},{24,408},{32,416},{40,424},{48,432},{56,4... | collective-permute-start | bytes 13448 | tf_op jit(solution)/shard_map/ppermute | solution.py:25
  23.3 15.8 %collective-permute-start = (f32[2,70,1,128]{1,3,2,0:T(8,128)S(1)}, f32[2,70,1,128]{1,3,2,0:T(8,128)S(1)}, u32[]{:S(2)}, u32[]{:S(2)}) collective-permute-start(f32[2,70,1,128]{1,3,2,0:T(8,128)S(1)} %get-tuple-element.37), channel_id=1, source_target_pairs={{0,8},{8,16},{16,24},{24,32},{32,40},{40,48},{48,56},{56,64},{64,7... | collective-permute-start | bytes 215048 | tf_op jit(solution)/shard_map/ppermute | solution.py:16
  26.5 13.2 %collective-permute-start.1 = (f32[2,70,1,128]{1,3,2,0:T(8,128)S(1)}, f32[2,70,1,128]{1,3,2,0:T(8,128)S(1)}, u32[]{:S(2)}, u32[]{:S(2)}) collective-permute-start(f32[2,70,1,128]{1,3,2,0:T(8,128)S(1)} %get-tuple-element.38), channel_id=1, source_target_pairs={{8,0},{16,8},{24,16},{32,24},{40,32},{48,40},{56,48},{64,56},{72,6... | collective-permute-start | bytes 215048 | tf_op jit(solution)/shard_map/ppermute | solution.py:17
  40.0 26.9 %collective-permute-start.8 = (f32[1,70,4,1]{1,3,2,0:T(1,128)S(1)}, f32[1,70,4,1]{1,3,2,0:T(1,128)S(1)}, u32[]{:S(2)}, u32[]{:S(2)}) collective-permute-start(f32[1,70,4,1]{1,3,2,0:T(1,128)S(1)} %get-tuple-element.57), channel_id=1, source_target_pairs={{0,1},{1,2},{2,3},{3,4},{4,5},{5,6},{6,7},{8,9},{9,10},{10,11},{11... | collective-permute-start | bytes 3368 | tf_op jit(solution)/shard_map/ppermute | solution.py:16
  44.1 22.8 %collective-permute-start.9 = (f32[1,70,4,1]{1,3,2,0:T(1,128)S(1)}, f32[1,70,4,1]{1,3,2,0:T(1,128)S(1)}, u32[]{:S(2)}, u32[]{:S(2)}) collective-permute-start(f32[1,70,4,1]{1,3,2,0:T(1,128)S(1)} %get-tuple-element.58), channel_id=1, source_target_pairs={{1,0},{2,1},{3,2},{4,3},{5,4},{6,5},{7,6},{9,8},{10,9},{11,10},{12... | collective-permute-start | bytes 3368 | tf_op jit(solution)/shard_map/ppermute | solution.py:17
  46.1 20.9 %collective-permute-start.7 = (f32[1,70,4,2]{1,3,2,0:T(2,128)S(1)}, f32[1,70,4,2]{1,3,2,0:T(2,128)S(1)}, u32[]{:S(2)}, u32[]{:S(2)}) collective-permute-start(f32[1,70,4,2]{1,3,2,0:T(2,128)S(1)} %pad_maximum_fusion.4), channel_id=1, source_target_pairs={{0,384},{8,392},{16,400},{24,408},{32,416},{40,424},{48,432},{56,4... | collective-permute-start | bytes 6728 | tf_op jit(solution)/shard_map/ppermute | solution.py:25
  52.0 15.1 %collective-permute-start.5 = (f32[1,70,1,128]{1,3,2,0:T(8,128)S(1)}, f32[1,70,1,128]{1,3,2,0:T(8,128)S(1)}, u32[]{:S(2)}, u32[]{:S(2)}) collective-permute-start(f32[1,70,1,128]{1,3,2,0:T(8,128)S(1)} %get-tuple-element.55), channel_id=1, source_target_pairs={{0,8},{8,16},{16,24},{24,32},{32,40},{40,48},{48,56},{56,64},{64,7... | collective-permute-start | bytes 107528 | tf_op jit(solution)/shard_map/ppermute | solution.py:16
  53.9 14.1 %collective-permute-start.6 = (f32[1,70,1,128]{1,3,2,0:T(8,128)S(1)}, f32[1,70,1,128]{1,3,2,0:T(8,128)S(1)}, u32[]{:S(2)}, u32[]{:S(2)}) collective-permute-start(f32[1,70,1,128]{1,3,2,0:T(8,128)S(1)} %get-tuple-element.56), channel_id=1, source_target_pairs={{8,0},{16,8},{24,16},{32,24},{40,32},{48,40},{56,48},{64,56},{72,6... | collective-permute-start | bytes 107528 | tf_op jit(solution)/shard_map/ppermute | solution.py:17
  181.5 22.8 %collective-permute-start.13 = (f32[1,70,4,1]{1,3,2,0:T(1,128)S(1)}, f32[1,70,4,1]{1,3,2,0:T(1,128)S(1)}, u32[]{:S(2)}, u32[]{:S(2)}) collective-permute-start(f32[1,70,4,1]{1,3,2,0:T(1,128)S(1)} %get-tuple-element.53), channel_id=1, source_target_pairs={{0,1},{1,2},{2,3},{3,4},{4,5},{5,6},{6,7},{8,9},{9,10},{10,11},{11... | collective-permute-start | bytes 3368 | tf_op jit(solution)/shard_map/ppermute | solution.py:16
  183.5 20.9 %collective-permute-start.14 = (f32[1,70,4,1]{1,3,2,0:T(1,128)S(1)}, f32[1,70,4,1]{1,3,2,0:T(1,128)S(1)}, u32[]{:S(2)}, u32[]{:S(2)}) collective-permute-start(f32[1,70,4,1]{1,3,2,0:T(1,128)S(1)} %get-tuple-element.54), channel_id=1, source_target_pairs={{1,0},{2,1},{3,2},{4,3},{5,4},{6,5},{7,6},{9,8},{10,9},{11,10},{12... | collective-permute-start | bytes 3368 | tf_op jit(solution)/shard_map/ppermute | solution.py:17
  185.9 18.5 %collective-permute-start.12 = (f32[1,70,4,2]{1,3,2,0:T(2,128)S(1)}, f32[1,70,4,2]{1,3,2,0:T(2,128)S(1)}, u32[]{:S(2)}, u32[]{:S(2)}) collective-permute-start(f32[1,70,4,2]{1,3,2,0:T(2,128)S(1)} %pad_maximum_fusion.5), channel_id=1, source_target_pairs={{0,384},{8,392},{16,400},{24,408},{32,416},{40,424},{48,432},{56,4... | collective-permute-start | bytes 6728 | tf_op jit(solution)/shard_map/ppermute | solution.py:25
  190.8 14.0 %collective-permute-start.10 = (f32[1,70,1,128]{1,3,2,0:T(8,128)S(1)}, f32[1,70,1,128]{1,3,2,0:T(8,128)S(1)}, u32[]{:S(2)}, u32[]{:S(2)}) collective-permute-start(f32[1,70,1,128]{1,3,2,0:T(8,128)S(1)} %get-tuple-element.51), channel_id=1, source_target_pairs={{0,8},{8,16},{16,24},{24,32},{32,40},{40,48},{48,56},{56,64},{64,7... | collective-permute-start | bytes 107528 | tf_op jit(solution)/shard_map/ppermute | solution.py:16
  192.7 13.1 %collective-permute-start.11 = (f32[1,70,1,128]{1,3,2,0:T(8,128)S(1)}, f32[1,70,1,128]{1,3,2,0:T(8,128)S(1)}, u32[]{:S(2)}, u32[]{:S(2)}) collective-permute-start(f32[1,70,1,128]{1,3,2,0:T(8,128)S(1)} %get-tuple-element.52), channel_id=1, source_target_pairs={{8,0},{16,8},{24,16},{32,24},{40,32},{48,40},{56,48},{64,56},{72,6... | collective-permute-start | bytes 107528 | tf_op jit(solution)/shard_map/ppermute | solution.py:17
  321.2 23.5 %collective-permute-start.18 = (f32[1,70,4,1]{1,3,2,0:T(1,128)S(1)}, f32[1,70,4,1]{1,3,2,0:T(1,128)S(1)}, u32[]{:S(2)}, u32[]{:S(2)}) collective-permute-start(f32[1,70,4,1]{1,3,2,0:T(1,128)S(1)} %get-tuple-element.49), channel_id=1, source_target_pairs={{0,1},{1,2},{2,3},{3,4},{4,5},{5,6},{6,7},{8,9},{9,10},{10,11},{11... | collective-permute-start | bytes 3368 | tf_op jit(solution)/shard_map/ppermute | solution.py:16
  323.2 21.5 %collective-permute-start.19 = (f32[1,70,4,1]{1,3,2,0:T(1,128)S(1)}, f32[1,70,4,1]{1,3,2,0:T(1,128)S(1)}, u32[]{:S(2)}, u32[]{:S(2)}) collective-permute-start(f32[1,70,4,1]{1,3,2,0:T(1,128)S(1)} %get-tuple-element.50), channel_id=1, source_target_pairs={{1,0},{2,1},{3,2},{4,3},{5,4},{6,5},{7,6},{9,8},{10,9},{11,10},{12... | collective-permute-start | bytes 3368 | tf_op jit(solution)/shard_map/ppermute | solution.py:17
  325.6 19.1 %collective-permute-start.17 = (f32[1,70,4,2]{1,3,2,0:T(2,128)S(1)}, f32[1,70,4,2]{1,3,2,0:T(2,128)S(1)}, u32[]{:S(2)}, u32[]{:S(2)}) collective-permute-start(f32[1,70,4,2]{1,3,2,0:T(2,128)S(1)} %pad_maximum_fusion.6), channel_id=1, source_target_pairs={{0,384},{8,392},{16,400},{24,408},{32,416},{40,424},{48,432},{56,4... | collective-permute-start | bytes 6728 | tf_op jit(solution)/shard_map/ppermute | solution.py:25
  331.1 14.4 %collective-permute-start.15 = (f32[1,70,1,128]{1,3,2,0:T(8,128)S(1)}, f32[1,70,1,128]{1,3,2,0:T(8,128)S(1)}, u32[]{:S(2)}, u32[]{:S(2)}) collective-permute-start(f32[1,70,1,128]{1,3,2,0:T(8,128)S(1)} %get-tuple-element.47), channel_id=1, source_target_pairs={{0,8},{8,16},{16,24},{24,32},{32,40},{40,48},{48,56},{56,64},{64,7... | collective-permute-start | bytes 107528 | tf_op jit(solution)/shard_map/ppermute | solution.py:16
  333.0 13.1 %collective-permute-start.16 = (f32[1,70,1,128]{1,3,2,0:T(8,128)S(1)}, f32[1,70,1,128]{1,3,2,0:T(8,128)S(1)}, u32[]{:S(2)}, u32[]{:S(2)}) collective-permute-start(f32[1,70,1,128]{1,3,2,0:T(8,128)S(1)} %get-tuple-element.48), channel_id=1, source_target_pairs={{8,0},{16,8},{24,16},{32,24},{40,32},{48,40},{56,48},{64,56},{72,6... | collective-permute-start | bytes 107528 | tf_op jit(solution)/shard_map/ppermute | solution.py:17
  461.2 22.2 %collective-permute-start.23 = (f32[1,70,4,1]{1,3,2,0:T(1,128)S(1)}, f32[1,70,4,1]{1,3,2,0:T(1,128)S(1)}, u32[]{:S(2)}, u32[]{:S(2)}) collective-permute-start(f32[1,70,4,1]{1,3,2,0:T(1,128)S(1)} %get-tuple-element.45), channel_id=1, source_target_pairs={{0,1},{1,2},{2,3},{3,4},{4,5},{5,6},{6,7},{8,9},{9,10},{10,11},{11... | collective-permute-start | bytes 3368 | tf_op jit(solution)/shard_map/ppermute | solution.py:16
  463.1 20.3 %collective-permute-start.24 = (f32[1,70,4,1]{1,3,2,0:T(1,128)S(1)}, f32[1,70,4,1]{1,3,2,0:T(1,128)S(1)}, u32[]{:S(2)}, u32[]{:S(2)}) collective-permute-start(f32[1,70,4,1]{1,3,2,0:T(1,128)S(1)} %get-tuple-element.46), channel_id=1, source_target_pairs={{1,0},{2,1},{3,2},{4,3},{5,4},{6,5},{7,6},{9,8},{10,9},{11,10},{12... | collective-permute-start | bytes 3368 | tf_op jit(solution)/shard_map/ppermute | solution.py:17
  465.5 17.9 %collective-permute-start.22 = (f32[1,70,4,2]{1,3,2,0:T(2,128)S(1)}, f32[1,70,4,2]{1,3,2,0:T(2,128)S(1)}, u32[]{:S(2)}, u32[]{:S(2)}) collective-permute-start(f32[1,70,4,2]{1,3,2,0:T(2,128)S(1)} %pad_maximum_fusion.7), channel_id=1, source_target_pairs={{0,384},{8,392},{16,400},{24,408},{32,416},{40,424},{48,432},{56,4... | collective-permute-start | bytes 6728 | tf_op jit(solution)/shard_map/ppermute | solution.py:25
  469.8 14.0 %collective-permute-start.20 = (f32[1,70,1,128]{1,3,2,0:T(8,128)S(1)}, f32[1,70,1,128]{1,3,2,0:T(8,128)S(1)}, u32[]{:S(2)}, u32[]{:S(2)}) collective-permute-start(f32[1,70,1,128]{1,3,2,0:T(8,128)S(1)} %get-tuple-element.43), channel_id=1, source_target_pairs={{0,8},{8,16},{16,24},{24,32},{32,40},{40,48},{48,56},{56,64},{64,7... | collective-permute-start | bytes 107528 | tf_op jit(solution)/shard_map/ppermute | solution.py:16
  (5 other events, 26.3 us)
where the time goes:
time: 598 us; the launch traced here: 597 us
  blocking collectives  440 us (74%)
  starting transfers between devices  129 us (22%)
  between operations  10.5 us (2%)
  other arithmetic  6.84 us (1%)
    psum x4, blocking collectives, reduce_all(): return lax.psum(terms, ('lon', 'lat'))  440 us
    ppermute x10, starting transfers between devices, padded(): after = lax.ppermute(leading, axis, down)  75.8 us
    ppermute x5, starting transfers between devices, shifted(): return lax.ppermute(value, axis, pairs)  28.3 us
    ppermute x10, starting transfers between devices, padded(): before = lax.ppermute(last, axis, up)  25.2 us
  transfers between devices with their start and end apart: 25, of which 10 were waited for; matrix products, arithmetic and copies ran while one was open for 0% of the time, Pallas kernels for 0%

commit v1 on v0

v1 whole, which is shorter than its diff:
```python
import jax
import jax.numpy as jnp
from jax import lax
from jax.experimental import pallas as pl
from jax.experimental.pallas import tpu as pltpu
from jax.sharding import PartitionSpec as P

MESH = pl.DeviceIdType.MESH
F32 = jnp.float32

LEV = 70
GROUP = 16
GROUPS = 5
PAD = GROUP * GROUPS
ROWS = 4
NX, NYH, NZ, NYL, NC = 4, 2, 12, 4, 2
NLONB, NBAND = NX * NYH * NZ, NYL * NC
SIZE_A, SIZE_B = NX * NYH * NYL, NZ * NC


def two_sum(a, b):
    s = a + b
    t = s - a
    return s, (a - (s - t)) + (b - t)


def quick_two_sum(a, b):
    s = a + b
    return s, b - (s - a)


def split(a):
    c = 4097.0 * a
    high = c - (c - a)
    return high, a - high


def two_prod(a, b):
    p = a * b
    ah, al = split(a)
    bh, bl = split(b)
    return p, ((ah * bh - p) + ah * bl + al * bh) + al * bl


def dd_add(a, b):
    s, e = two_sum(a[0], b[0])
    return quick_two_sum(s, e + (a[1] + b[1]))


def dd_neg(a):
    return -a[0], -a[1]


def dd_sub(a, b):
    return dd_add(a, dd_neg(b))


def dd_mul(a, b):
    p, e = two_prod(a[0], b[0])
    return quick_two_sum(p, e + (a[0] * b[1] + a[1] * b[0]))


def dd_div(a, b):
    q = a[0] / b[0]
    zero = jnp.zeros_like(q)
    r = dd_sub(a, dd_mul((q, zero), b))
    return quick_two_sum(q, r[0] / b[0])


def roll(x, shift, axis):
    return pltpu.roll(x, shift % x.shape[axis], axis)


def halo_peers():
    lon, band = lax.axis_index("lon"), lax.axis_index("lat")
    west, east = lax.rem(lon + NLONB - 1, NLONB), lax.rem(lon + 1, NLONB)
    first = 1 - jnp.minimum(band, 1)
    last = jnp.maximum(band, NBAND - 2) - (NBAND - 2)

    def across(index, pole):
        return lax.rem(index + pole * (NLONB // 2), NLONB)

    left_band, right_band = band - 1 + first, band + 1 - last
    beside = ((west, band), (east, band))
    left = tuple((across(i, first), left_band) for i in (lon, west, east))
    right = tuple((across(i, last), right_band) for i in (lon, west, east))
    return beside, left, right, first, last


def sum_peers():
    lon, band = lax.axis_index("lon"), lax.axis_index("lat")
    x, y_hi, z = lax.rem(lon, NX), lax.rem(lon // NX, NYH), lon // (NX * NYH)
    core, y_lo = lax.rem(band, NC), band // NC
    me_a = (y_hi * NYL + y_lo) * NX + x
    me_b = z * NC + core
    group_a, group_b = [], []
    for j in range(1, SIZE_A):
        t = lax.rem(me_a + j, SIZE_A)
        px, py = lax.rem(t, NX), t // NX
        group_a.append(((z * NYH + py // NYL) * NX + px, lax.rem(py, NYL) * NC + core))
    for j in range(1, SIZE_B):
        t = lax.rem(me_b + j, SIZE_B)
        pc, pz = lax.rem(t, NC), t // NC
        group_b.append(((pz * NYH + y_hi) * NX + x, y_lo * NC + pc))
    return (me_a, group_a), (me_b, group_b)


def kernel(
    b_hbm, x_hbm, d_hbm, h_hbm, vc, sol_hbm, res_hbm,
    b_in, x_in, d_in, h_in, d_c, h_c, d_o, h_o,
    q_a, q_b, q_c, q_d, o_a, o_b,
    near, wide, vs, packed, ext1, ext2, ex, ey, sums_a, sums_b, row_a, row_b, couple, sol, res,
    load_sem, send1, recv1, send1x, recv1x, send2, recv2, send2x, recv2x, send_a, recv_a, send_b, recv_b,
):
    beside, left, right, first, last = halo_peers()
    (me_a, group_a), (me_b, group_b) = sum_peers()

    loads = [
        pltpu.make_async_copy(src, dst.at[pl.ds(0, LEV), pl.ds(2, ROWS)], load_sem.at[i])
        for i, (src, dst) in enumerate(((d_hbm, d_in), (x_hbm, x_in), (h_hbm, h_in), (b_hbm, b_in)))
    ]
    for copy in loads:
        copy.start()

    barrier = pltpu.get_barrier_semaphore()
    peers = [*beside, *left, *right, *group_a, *group_b]
    for peer in peers:
        pl.semaphore_signal(barrier, inc=1, device_id=peer, device_id_type=MESH)

    lane = lax.broadcasted_iota(jnp.int32, (8, 128), 1)
    sub = lax.broadcasted_iota(jnp.int32, (8, 128), 0)
    lane5 = lax.broadcasted_iota(jnp.int32, (GROUPS, 8, 128), 2)
    sub5 = lax.broadcasted_iota(jnp.int32, (GROUPS, 8, 128), 1)
    col5 = lax.rem(lane5, 8)
    is_own = (sub >= 2) & (sub < 6)

    tail = jnp.zeros((PAD - LEV, 8, 128), F32)
    for ref in (b_in, x_in, d_in, h_in, near):
        ref[LEV:PAD] = tail
    for i in range(3):
        for j in range(2):
            wide[i, j, LEV:PAD] = tail
    for ref in (q_a, q_b, q_c, q_d, o_a, o_b):
        ref[0] = jnp.zeros((8, 128), F32)
        ref[PAD + 1] = jnp.zeros((8, 128), F32)

    for k in range(PAD + 2):
        couple[k] = vc[k - 1] if 1 <= k < LEV else jnp.float32(0.0)

    def levels(step, init):
        def group(p, carry):
            return step(p, carry)

        return lax.fori_loop(0, GROUPS, group, init)

    def pack_in(tile, value, i):
        return jnp.where((lane >= 8 * i) & (lane < 8 * i + 8), roll(value, 8 * i + 4, 1), tile)

    def pack_field(ref, slot, at):
        def step(p, _):
            tile = jnp.zeros((8, 128), F32)
            for i in range(GROUP):
                tile = pack_in(tile, ref[p * GROUP + i + at], i)
            packed[slot, p] = tile
            return 0

        levels(step, 0)

    loads[0].wait()
    loads[1].wait()

    def scaled_guess(p, _):
        tile = jnp.zeros((8, 128), F32)
        for i in range(GROUP):
            k = p * GROUP + i
            value = d_in[k] * x_in[k]
            q_a[k + 1] = value
            tile = pack_in(tile, value, i)
        packed[0, p] = tile
        return 0

    levels(scaled_guess, 0)

    def remote(src, dst, send, recv, peer):
        copy = pltpu.make_async_remote_copy(
            src_ref=src, dst_ref=dst, send_sem=send, recv_sem=recv, device_id=peer, device_id_type=MESH
        )
        copy.start()
        sends.append(copy)

    def landed(ref, sem):
        pltpu.make_async_copy(ref, ref, sem).wait()

    sends = []
    pl.semaphore_wait(barrier, len(peers))

    lev = pl.ds(0, LEV)
    lev1 = pl.ds(1, LEV)
    (west, east) = beside
    left_side, right_side = 1 - first, last
    remote(q_a.at[lev1, pl.ds(5, 1)], near.at[lev, pl.ds(5, 1)], send1.at[0], recv1.at[0], east)
    remote(q_a.at[lev1, pl.ds(2, 1)], near.at[lev, pl.ds(2, 1)], send1.at[1], recv1.at[1], west)
    remote(packed.at[0], ext1.at[left_side], send1x.at[0], recv1x.at[left_side], left[0])
    remote(packed.at[0], ext1.at[right_side], send1x.at[1], recv1x.at[right_side], right[0])

    def send_packed(slot):
        for j in range(3):
            at = (0, 2, 1)[j]
            remote(packed.at[slot + 1], ext2.at[slot, left_side, at], send2x.at[slot, 0, j],
                   recv2x.at[slot, left_side, at], left[j])
            remote(packed.at[slot + 1], ext2.at[slot, right_side, at], send2x.at[slot, 1, j],
                   recv2x.at[slot, right_side, at], right[j])

    pack_field(d_in, 1, 0)
    loads[2].wait()
    pack_field(h_in, 2, 0)
    for slot, ref in ((0, d_in), (1, h_in)):
        remote(ref.at[lev, pl.ds(3, 3)], wide.at[slot, 0, lev, pl.ds(3, 3)], send2.at[slot, 0], recv2.at[slot, 0], east)
        remote(ref.at[lev, pl.ds(2, 3)], wide.at[slot, 1, lev, pl.ds(2, 3)], send2.at[slot, 1], recv2.at[slot, 1], west)
        send_packed(slot)

    for p in range(GROUPS):
        below = jnp.zeros((8, 128), F32)
        above = jnp.zeros((8, 128), F32)
        for i in range(GROUP):
            k = p * GROUP + i
            here = (lane >= 8 * i) & (lane < 8 * i + 8)
            below = jnp.where(here, couple[k + 1], below)
            above = jnp.where(here, couple[k], above)
        ey[1, p] = below
        ey[2, p] = above

    def mirrored(value, side):
        if side == 0:
            out = roll(value, -1, 2)
            for c, s in ((0, -7), (1, -5), (2, -3)):
                out = jnp.where(col5 == c, roll(value, s, 2), out)
            return jnp.where(jnp.full(value.shape, first, jnp.int32) == 1, out, value)
        out = roll(value, 1, 2)
        for c, s in ((5, 3), (6, 5), (7, 7)):
            out = jnp.where(col5 == c, roll(value, s, 2), out)
        return jnp.where(jnp.full(value.shape, last, jnp.int32) == 1, out, value)

    def both_sides(part):
        return jnp.where(col5 < 4, mirrored(part(0), 0), mirrored(part(1), 1))

    def ring_center(slot):
        def part(side):
            lo, hi = roll(ext2[slot, side, 1], 4, 1), roll(ext2[slot, side, 2], 4, 1)
            return jnp.where(sub5 < 2, lo, jnp.where(sub5 >= 6, hi, ext2[slot, side, 0]))

        return both_sides(part)

    def ring_outer(slot):
        def part(side):
            lo, hi = roll(ext2[slot, side, 1], 4, 1), roll(ext2[slot, side, 2], 4, 1)
            return jnp.where(sub5 < 2, hi, lo)

        return both_sides(part)

    def edges(value):
        return jnp.where(col5 == 3, roll(value, -1, 2), roll(value, 1, 2))

    def lat_sum(q, edge, i):
        e = roll(edge, 124 - 8 * i, 1)
        return jnp.where(lane == 0, e, roll(q, 1, 1)) + jnp.where(lane == 127, e, roll(q, -1, 1))

    def stencil(q, up, down, h4, lon_sum, lat, k):
        flux = couple[k + 1] * (q - down) - couple[k] * (up - q)
        return h4 * q - lon_sum - lat + flux

    landed(near.at[lev, pl.ds(5, 1)], recv1.at[0])
    landed(near.at[lev, pl.ds(2, 1)], recv1.at[1])
    landed(ext1.at[0], recv1x.at[0])
    landed(ext1.at[1], recv1x.at[1])
    ey[0] = edges(both_sides(lambda side: ext1[side]))
    loads[3].wait()

    def first_residual(p, acc):
        tile = jnp.zeros((8, 128), F32)
        edge = ey[0, p]
        for i in range(GROUP):
            k = p * GROUP + i
            q = q_a[k + 1]
            n = roll(near[k], 4, 0)
            lon_sum = roll(jnp.where(sub == 6, n, q), -1, 0) + roll(jnp.where(sub == 1, n, q), 1, 0)
            d = d_in[k]
            t = stencil(q, q_a[k], q_a[k + 2], 4.0 + h_in[k], lon_sum, lat_sum(q, edge, i), k)
            r = b_in[k] - d * t
            vs[0, k] = r
            acc = acc + r * r
            value = d * r
            q_b[k + 1] = value
            tile = pack_in(tile, value, i)
        packed[3, p] = tile
        return acc

    zero = jnp.zeros((8, 128), F32)
    moments = [levels(first_residual, zero)]

    remote(q_b.at[lev1, pl.ds(2, ROWS)], wide.at[2, 0, lev, pl.ds(2, ROWS)], send2.at[2, 0], recv2.at[2, 0], east)
    remote(q_b.at[lev1, pl.ds(2, ROWS)], wide.at[2, 1, lev, pl.ds(2, ROWS)], send2.at[2, 1], recv2.at[2, 1], west)
    send_packed(2)

    def wait_ring(slot):
        east_rows, west_rows = (pl.ds(3, 3), pl.ds(2, 3)) if slot < 2 else (pl.ds(2, ROWS),) * 2
        landed(wide.at[slot, 0, lev, east_rows], recv2.at[slot, 0])
        landed(wide.at[slot, 1, lev, west_rows], recv2.at[slot, 1])
        for side in range(2):
            for j in range(3):
                landed(ext2.at[slot, side, j], recv2x.at[slot, side, j])

    def gather(slot, ref, at, center, outer, center_at, plus):
        def step(p, _):
            for i in range(GROUP):
                k = p * GROUP + i
                w, e = roll(wide[slot, 0, k], 4, 0), roll(wide[slot, 1, k], 4, 0)
                mine = ref[k + at]
                center[k + center_at] = jnp.where(sub < 2, w, jnp.where(sub >= 6, e, mine)) + plus
                outer[k + center_at] = jnp.where(sub < 2, e, w) + plus
            return 0

        levels(step, 0)

    for slot, ref, center, outer, plus in ((0, d_in, d_c, d_o, 0.0), (1, h_in, h_c, h_o, 4.0)):
        wait_ring(slot)
        gather(slot, ref, 0, center, outer, 0, plus)
        ex[slot] = ring_center(slot) + plus
    wait_ring(2)
    gather(2, q_b, 1, q_c, o_a, 1, 0.0)
    ring = ring_center(2)
    ring_o = ring_outer(2)
    ey[0] = edges(ring)
    ey[3] = edges(ring_o)

    def ring_step(x, edge_tiles, outer):
        right_of = roll(jnp.where(col5 == 4, edge_tiles, x), -1, 2)
        left_of = roll(jnp.where(col5 == 3, edge_tiles, x), 1, 2)
        o = x if outer is None else outer
        lon_sum = roll(jnp.where(sub5 == 0, o, x), -1, 1) + roll(jnp.where(sub5 == 7, o, x), 1, 1)
        ahead, behind = roll(x, -8, 2), roll(x, 8, 2)
        none = jnp.zeros((1, 8, 128), F32)
        down = jnp.where(lane5 >= 120, jnp.concatenate([ahead[1:], none]), ahead)
        up = jnp.where(lane5 < 8, jnp.concatenate([none, behind[:-1]]), behind)
        t = ex[1] * x - lon_sum - (left_of + right_of) + (ey[1] * (x - down) - ey[2] * (up - x))
        d = ex[0]
        return d * (d * t)

    def apply(n, src, dst, out_src, out_dst, slot):
        def step(p, acc):
            even, odd = acc
            tile = jnp.zeros((8, 128), F32)
            edge = ey[0, p]
            edge_o = ey[3, p]
            for i in range(GROUP):
                k = p * GROUP + i
                q = src[k + 1]
                o = q if out_src is None else out_src[k + 1]
                lon_sum = roll(jnp.where(sub == 0, o, q), -1, 0) + roll(jnp.where(sub == 7, o, q), 1, 0)
                d = d_c[k]
                v = d * stencil(q, src[k], src[k + 2], h_c[k], lon_sum, lat_sum(q, edge, i), k)
                vs[n, k] = v
                odd = odd + vs[n - 1, k] * v
                even = even + v * v
                if dst is not None:
                    value = d * v
                    dst[k + 1] = value
                    tile = pack_in(tile, value, i)
                if out_dst is not None:
                    lon_o = roll(jnp.where(sub == 0, q, o), -1, 0) + roll(jnp.where(sub == 7, q, o), 1, 0)
                    do = d_o[k]
                    to = stencil(o, out_src[k], out_src[k + 2], h_o[k], lon_o, lat_sum(o, edge_o, i), k)
                    out_dst[k + 1] = do * (do * to)
            if dst is not None:
                ex[slot, p] = tile
            return even, odd

        even, odd = levels(step, (zero, zero))
        moments.extend([odd, even])

    def pack_ref(ref, slot):
        def step(p, _):
            tile = jnp.zeros((8, 128), F32)
            for i in range(GROUP):
                tile = pack_in(tile, ref[p * GROUP + i + 1], i)
            ex[slot, p] = tile
            return 0

        levels(step, 0)

    pack_ref(q_c, 2)
    apply(1, q_c, q_d, o_a, o_b, 3)
    ring = ring_step(ring, ex[2], ring_o)
    ey[0] = edges(ring)
    apply(2, q_d, q_c, o_b, None, 2)
    ring = ring_step(ring, ex[3], None)
    ey[0] = edges(ring)
    apply(3, q_c, q_d, None, None, 3)
    ring = ring_step(ring, ex[2], None)
    ey[0] = edges(ring)
    apply(4, q_d, None, None, None, 2)

    def total(acc):
        value = jnp.where(is_own, acc, 0.0)
        pair = two_sum(value, roll(value, -2, 0))
        return dd_add(pair, tuple(roll(part, -1, 0) for part in pair))

    pairs = [total(acc) for acc in moments]
    row = jnp.zeros((8, 128), F32)
    for start in (0, 8):
        high, low = zero, zero
        for k in range(start, min(start + 8, len(pairs))):
            shift = k - start - 2
            high = jnp.where(sub == k - start, roll(pairs[k][0], shift, 0), high)
            low = jnp.where(sub == k - start, roll(pairs[k][1], shift, 0), low)
        pair = (high, low)
        for width in (64, 32, 16, 8, 4, 2, 1):
            pair = dd_add(pair, tuple(roll(part, width, 1) for part in pair))
        row = row + jnp.where(lane == sub + start, pair[0], 0.0) + jnp.where(lane == sub + start + 16, pair[1], 0.0)
    for width in (4, 2, 1):
        row = row + roll(row, width, 0)

    def sum_over(row, line, slots, me, group, size, send, recv):
        line[...] = row
        slots[pl.ds(me, 1), :] = row[0:1]
        for peer in group:
            copy = pltpu.make_async_remote_copy(
                src_ref=line.at[pl.ds(0, 1)], dst_ref=slots.at[pl.ds(me, 1)], send_sem=send.at[0],
                recv_sem=recv.at[0], device_id=peer, device_id_type=MESH,
            )
            copy.start()
        landed(slots.at[pl.ds(0, size - 1)], recv.at[0])
        parts = [(slots[8 * j : 8 * j + 8], zero) for j in range(size // 8)]
        while len(parts) > 1:
            parts = [
                dd_add_raw(parts[j], parts[j + 1]) if j + 1 < len(parts) else parts[j] for j in range(0, len(parts), 2)
            ]
        pair = parts[0]
        for width in (4, 2, 1):
            pair = dd_add_raw(pair, tuple(roll(part, width, 0) for part in pair))
        low = pair[1] + roll(pair[0], -16, 1)
        high, low = quick_two_sum(pair[0], low)
        return jnp.where(lane < 16, high, jnp.where(lane < 32, roll(low, 16, 1), 0.0))

    def dd_add_raw(a, b):
        s, e = two_sum(a[0], b[0])
        return s, e + (a[1] + b[1])

    row = sum_over(row, row_a, sums_a, me_a, group_a, SIZE_A, send_a, recv_a)
    row = sum_over(row, row_b, sums_b, me_b, group_b, SIZE_B, send_b, recv_b)

    m = (row, roll(row, -16, 1))

    def at(pair, k):
        return tuple(jnp.broadcast_to(part[:, k : k + 1], (8, 128)) for part in pair)

    def ahead(pair, k):
        return tuple(roll(part, -k, 1) for part in pair)

    one = (jnp.ones((8, 128), F32), zero)
    m0, m1, m2, m3 = (at(m, k) for k in range(4))
    alpha = dd_div(m0, m1)
    g = dd_sub(m, dd_mul(alpha, ahead(m, 1)))
    t = dd_sub(g, dd_mul(alpha, ahead(g, 1)))
    omega = dd_div(at(t, 1), at(t, 2))
    rho = dd_sub(at(g, 0), dd_mul(omega, at(g, 1)))
    beta = dd_mul(dd_div(rho, m0), dd_div(alpha, omega))
    both = dd_add(alpha, omega)
    d0 = dd_add(one, beta)
    d1 = dd_neg(dd_add(both, dd_mul(beta, omega)))
    d2 = dd_mul(alpha, omega)
    image = dd_add(dd_add(dd_mul(d0, m1), dd_mul(d1, m2)), dd_mul(d2, m3))
    alpha1 = dd_div(rho, image)
    h1 = dd_neg(dd_add(both, dd_mul(alpha1, d0)))
    h2 = dd_sub(d2, dd_mul(alpha1, d1))
    h3 = dd_neg(dd_mul(alpha1, d2))

    def half_with(pair):
        out = pair
        for j, h in ((1, h1), (2, h2), (3, h3)):
            out = dd_add(out, dd_mul(h, ahead(pair, j)))
        return out

    t = half_with(half_with(m))
    omega1 = dd_div(at(t, 1), at(t, 2))
    res_c = (
        one,
        dd_sub(h1, omega1),
        dd_sub(h2, dd_mul(omega1, h1)),
        dd_sub(h3, dd_mul(omega1, h2)),
        dd_neg(dd_mul(omega1, h3)),
    )
    sol_c = (
        dd_add(dd_add(both, dd_mul(alpha1, d0)), omega1),
        dd_add(dd_sub(dd_mul(alpha1, d1), d2), dd_mul(omega1, h1)),
        dd_add(dd_mul(alpha1, d2), dd_mul(omega1, h2)),
        dd_mul(omega1, h3),
    )

    def finish(p, _):
        for i in range(GROUP):
            k = p * GROUP + i
            v = [vs[n, k] for n in range(5)]
            sol[k] = x_in[k] + (sol_c[0][0] * v[0] + sol_c[1][0] * v[1] + sol_c[2][0] * v[2] + sol_c[3][0] * v[3])
            res[k] = v[0] + (res_c[1][0] * v[1] + res_c[2][0] * v[2] + res_c[3][0] * v[3] + res_c[4][0] * v[4])
        return 0

    levels(finish, 0)
    stores = [
        pltpu.make_async_copy(src.at[lev, pl.ds(2, ROWS)], dst, load_sem.at[i])
        for i, (src, dst) in enumerate(((sol, sol_hbm), (res, res_hbm)))
    ]
    for copy in stores:
        copy.start()
    for copy in sends:
        copy.wait_send()
    landed(sums_a.at[pl.ds(0, SIZE_A - 1)], send_a.at[0])
    landed(sums_b.at[pl.ds(0, SIZE_B - 1)], send_b.at[0])
    for copy in stores:
        copy.wait()


def body(right_side, first_guess, cell_scale, helmholtz_term, vertical_coupling):
    block = jax.ShapeDtypeStruct((LEV, ROWS, 128), F32)
    field = pltpu.VMEM((PAD, 8, 128), F32)
    guarded = pltpu.VMEM((PAD + 2, 8, 128), F32)
    dma = pltpu.SemaphoreType.DMA
    return pl.pallas_call(
        kernel,
        out_shape=(block, block),
        in_specs=[pl.BlockSpec(memory_space=pl.ANY)] * 4 + [pl.BlockSpec(memory_space=pltpu.SMEM)],
        out_specs=(pl.BlockSpec(memory_space=pl.ANY),) * 2,
        scratch_shapes=[
            *[field] * 8,
            *[guarded] * 6,
            field,
            pltpu.VMEM((3, 2, PAD, 8, 128), F32),
            pltpu.VMEM((5, PAD, 8, 128), F32),
            pltpu.VMEM((4, GROUPS, 8, 128), F32),
            pltpu.VMEM((2, GROUPS, 8, 128), F32),
            pltpu.VMEM((3, 2, 3, GROUPS, 8, 128), F32),
            pltpu.VMEM((4, GROUPS, 8, 128), F32),
            pltpu.VMEM((4, GROUPS, 8, 128), F32),
            pltpu.VMEM((SIZE_A, 128), F32),
            pltpu.VMEM((SIZE_B, 128), F32),
            pltpu.VMEM((8, 128), F32),
            pltpu.VMEM((8, 128), F32),
            pltpu.SMEM((PAD + 2,), F32),
            field,
            field,
            dma((4,)),
            dma((2,)),
            dma((2,)),
            dma((2,)),
            dma((2,)),
            dma((3, 2)),
            dma((3, 2)),
            dma((3, 2, 3)),
            dma((3, 2, 3)),
            *[dma((1,))] * 4,
        ],
        compiler_params=pltpu.CompilerParams(collective_id=0, has_side_effects=True, vmem_limit_bytes=48 << 20),
        cost_estimate=pl.CostEstimate(flops=8_000_000, bytes_accessed=900_000, transcendentals=0),
    )(right_side, first_guess, cell_scale, helmholtz_term, vertical_coupling)


def solution(mesh):
    spec = P(None, "lon", "lat")
    return jax.shard_map(
        body, mesh=mesh, in_specs=(spec, spec, spec, spec, P()), out_specs=(spec, spec), check_vma=False
    )
```

time: 598 us -> 75.8 us (0.13)
  blocking collectives: 440 us -> 0 us
  starting transfers between devices: 129 us -> 0 us
  Pallas kernels: 0 us -> 69.4 us
  between operations: 10.5 us -> 0.65 us
  other arithmetic: 6.84 us -> 0 us
    psum x4 -> x0, blocking collectives: 440 us -> none  [reduce_all(): return lax.psum(terms, ('lon', 'lat'))]
    ppermute x25 -> x0, starting transfers between devices: 129 us -> none  [the longest x10 75.8 us: padded(): after = lax.ppermute(leading, axis, down)]
    pallas_call x0 -> x1, Pallas kernels: none -> 69.4 us  [body(): pl.pallas_call(kernel, out_shape=(block, block), in_specs=[pl.BlockSpec(m...]
  transfers between devices with their start and end apart: 25 -> 0, of which waited for: 10 -> 0; matrix products, arithmetic and copies ran while one was open for 0% -> 0% of each run, Pallas kernels for 0% -> 0%
where the time goes in v1:
time: 75.8 us; the launch traced here: 75.6 us
  Pallas kernels  69.4 us (92%)
  local copies, waits for them, and re-layouts  5.6 us (7%)
    pallas_call x1, Pallas kernels, body(): pl.pallas_call(kernel, out_shape=(block, block), in_specs=[pl.BlockSpec(m...  69.4 us
    unnamed x12, local copies, waits for them, and re-layouts  5.6 us

profile of v1, /device:TPU:1, one launch (start us, length us, event | category | flops | bytes accessed | tf_op | source)
XLA Modules:
  0.0 75.6 jit_solution(14698426000324518971)
XLA Ops:
  0.6 0.0 copy-start
  0.6 0.9 %copy-done = f32[70,4,128]{2,1,0:T(4,128)S(1)} copy-done((f32[70,4,128]{2,1,0:T(4,128)S(1)}, f32[70,4,128]{2,1,0:T(4,128)}, u32[]{:S(2)}) %copy-start) | copy-done | bytes 143384
  1.5 0.0 copy-start.1
  1.5 0.9 %copy-done.1 = f32[70,4,128]{2,1,0:T(4,128)S(1)} copy-done((f32[70,4,128]{2,1,0:T(4,128)S(1)}, f32[70,4,128]{2,1,0:T(4,128)}, u32[]{:S(2)}) %copy-start.1) | copy-done | bytes 143384
  2.4 0.0 copy-start.2
  2.5 0.9 %copy-done.2 = f32[70,4,128]{2,1,0:T(4,128)S(1)} copy-done((f32[70,4,128]{2,1,0:T(4,128)S(1)}, f32[70,4,128]{2,1,0:T(4,128)}, u32[]{:S(2)}) %copy-start.2) | copy-done | bytes 143384
  3.4 0.0 copy-start.3
  3.4 0.9 %copy-done.3 = f32[70,4,128]{2,1,0:T(4,128)S(1)} copy-done((f32[70,4,128]{2,1,0:T(4,128)S(1)}, f32[70,4,128]{2,1,0:T(4,128)}, u32[]{:S(2)}) %copy-start.3) | copy-done | bytes 143384
  4.3 0.0 copy-start.4
  4.3 0.7 copy-done.4
  4.9 69.4 %shard_map.68 = (f32[70,4,128]{2,1,0:T(4,128)S(1)}, f32[70,4,128]{2,1,0:T(4,128)S(1)}) custom-call(f32[70,4,128]{2,1,0:T(4,128)S(1)} %copy-done, f32[70,4,128]{2,1,0:T(4,128)S(1)} %copy-done.1, f32[70,4,128]{2,1,0:T(4,128)S(1)} %copy-done.2, f32[70,4,128]{2,1,0:T(4,128)S(1)} %copy-done.3, f32[69]{0:T(128)S(1)} %copy-done.4), custom_call_target="tpu_custom_call" | custom-call | flops 8000000 | bytes 900000 | tf_op jit(solution)/shard_map/pallas_call | solution.py:528
  74.3 0.7 copy.9
  75.0 0.7 copy.10
Async XLA Ops:
  0.6 0.9 %copy-start = (f32[70,4,128]{2,1,0:T(4,128)S(1)}, f32[70,4,128]{2,1,0:T(4,128)}, u32[]{:S(2)}) copy-start(f32[70,4,128]{2,1,0:T(4,128)} %b_hbm.1) | copy-start | bytes 430084
  1.5 0.9 %copy-start.1 = (f32[70,4,128]{2,1,0:T(4,128)S(1)}, f32[70,4,128]{2,1,0:T(4,128)}, u32[]{:S(2)}) copy-start(f32[70,4,128]{2,1,0:T(4,128)} %x_hbm.1) | copy-start | bytes 430084
  2.4 0.9 %copy-start.2 = (f32[70,4,128]{2,1,0:T(4,128)S(1)}, f32[70,4,128]{2,1,0:T(4,128)}, u32[]{:S(2)}) copy-start(f32[70,4,128]{2,1,0:T(4,128)} %d_hbm.1) | copy-start | bytes 430084
  3.4 0.9 %copy-start.3 = (f32[70,4,128]{2,1,0:T(4,128)S(1)}, f32[70,4,128]{2,1,0:T(4,128)}, u32[]{:S(2)}) copy-start(f32[70,4,128]{2,1,0:T(4,128)} %h_hbm.1) | copy-start | bytes 430084
  4.3 0.7 copy-start.4

commit v2 on v1

--- a/solution.py
+++ b/solution.py
@@ -106,10 +106,10 @@
 
 
 def kernel(
-    b_hbm, x_hbm, d_hbm, h_hbm, vc, sol_hbm, res_hbm,
+    b_hbm, x_hbm, d_hbm, h_hbm, vc_hbm, sol_hbm, res_hbm,
     b_in, x_in, d_in, h_in, d_c, h_c, d_o, h_o,
     q_a, q_b, q_c, q_d, o_a, o_b,
-    near, wide, vs, packed, ext1, ext2, ex, ey, sums_a, sums_b, row_a, row_b, couple, sol, res,
+    near, wide, vs, packed, ext1, ext2, ex, ey, sums_a, sums_b, row_a, row_b, vc, couple, sol, res,
     load_sem, send1, recv1, send1x, recv1x, send2, recv2, send2x, recv2x, send_a, recv_a, send_b, recv_b,
 ):
     beside, left, right, first, last = halo_peers()
@@ -119,6 +119,7 @@
         pltpu.make_async_copy(src, dst.at[pl.ds(0, LEV), pl.ds(2, ROWS)], load_sem.at[i])
         for i, (src, dst) in enumerate(((d_hbm, d_in), (x_hbm, x_in), (h_hbm, h_in), (b_hbm, b_in)))
     ]
+    loads.append(pltpu.make_async_copy(vc_hbm, vc, load_sem.at[4]))
     for copy in loads:
         copy.start()
 
@@ -132,6 +133,7 @@
     lane5 = lax.broadcasted_iota(jnp.int32, (GROUPS, 8, 128), 2)
     sub5 = lax.broadcasted_iota(jnp.int32, (GROUPS, 8, 128), 1)
     col5 = lax.rem(lane5, 8)
+    lane8 = lane // 8
     is_own = (sub >= 2) & (sub < 6)
 
     tail = jnp.zeros((PAD - LEV, 8, 128), F32)
@@ -144,9 +146,6 @@
         ref[0] = jnp.zeros((8, 128), F32)
         ref[PAD + 1] = jnp.zeros((8, 128), F32)
 
-    for k in range(PAD + 2):
-        couple[k] = vc[k - 1] if 1 <= k < LEV else jnp.float32(0.0)
-
     def levels(step, init):
         def group(p, carry):
             return step(p, carry)
@@ -154,7 +153,7 @@
         return lax.fori_loop(0, GROUPS, group, init)
 
     def pack_in(tile, value, i):
-        return jnp.where((lane >= 8 * i) & (lane < 8 * i + 8), roll(value, 8 * i + 4, 1), tile)
+        return jnp.where(lane8 == i, roll(value, 8 * i + 4, 1), tile)
 
     def pack_field(ref, slot, at):
         def step(p, _):
@@ -200,31 +199,41 @@
     left_side, right_side = 1 - first, last
     remote(q_a.at[lev1, pl.ds(5, 1)], near.at[lev, pl.ds(5, 1)], send1.at[0], recv1.at[0], east)
     remote(q_a.at[lev1, pl.ds(2, 1)], near.at[lev, pl.ds(2, 1)], send1.at[1], recv1.at[1], west)
-    remote(packed.at[0], ext1.at[left_side], send1x.at[0], recv1x.at[left_side], left[0])
-    remote(packed.at[0], ext1.at[right_side], send1x.at[1], recv1x.at[right_side], right[0])
+    mine = (slice(None), pl.ds(2, ROWS))
+    remote(packed.at[0, *mine], ext1.at[left_side, *mine], send1x.at[0], recv1x.at[left_side], left[0])
+    remote(packed.at[0, *mine], ext1.at[right_side, *mine], send1x.at[1], recv1x.at[right_side], right[0])
+
+    def ring_rows(slot, at):
+        deep = 2 if slot < 2 else 3
+        return slice(None), (pl.ds(2, ROWS), pl.ds(6 - deep, deep), pl.ds(2, deep))[at]
 
     def send_packed(slot):
-        for j in range(3):
+        for j in (1, 2, 0):
             at = (0, 2, 1)[j]
-            remote(packed.at[slot + 1], ext2.at[slot, left_side, at], send2x.at[slot, 0, j],
+            rows = ring_rows(slot, at)
+            remote(packed.at[slot + 1, *rows], ext2.at[slot, left_side, at, *rows], send2x.at[slot, 0, j],
                    recv2x.at[slot, left_side, at], left[j])
-            remote(packed.at[slot + 1], ext2.at[slot, right_side, at], send2x.at[slot, 1, j],
+            remote(packed.at[slot + 1, *rows], ext2.at[slot, right_side, at, *rows], send2x.at[slot, 1, j],
                    recv2x.at[slot, right_side, at], right[j])
 
-    pack_field(d_in, 1, 0)
     loads[2].wait()
-    pack_field(h_in, 2, 0)
     for slot, ref in ((0, d_in), (1, h_in)):
         remote(ref.at[lev, pl.ds(3, 3)], wide.at[slot, 0, lev, pl.ds(3, 3)], send2.at[slot, 0], recv2.at[slot, 0], east)
         remote(ref.at[lev, pl.ds(2, 3)], wide.at[slot, 1, lev, pl.ds(2, 3)], send2.at[slot, 1], recv2.at[slot, 1], west)
+    for slot, ref in ((0, d_in), (1, h_in)):
+        pack_field(ref, slot + 1, 0)
         send_packed(slot)
+
+    loads[4].wait()
+    for k in range(PAD + 2):
+        couple[k] = vc[k - 1] if 1 <= k < LEV else jnp.float32(0.0)
 
     for p in range(GROUPS):
         below = jnp.zeros((8, 128), F32)
         above = jnp.zeros((8, 128), F32)
         for i in range(GROUP):
             k = p * GROUP + i
-            here = (lane >= 8 * i) & (lane < 8 * i + 8)
+            here = lane8 == i
             below = jnp.where(here, couple[k + 1], below)
             above = jnp.where(here, couple[k], above)
         ey[1, p] = below
@@ -271,8 +280,8 @@
 
     landed(near.at[lev, pl.ds(5, 1)], recv1.at[0])
     landed(near.at[lev, pl.ds(2, 1)], recv1.at[1])
-    landed(ext1.at[0], recv1x.at[0])
-    landed(ext1.at[1], recv1x.at[1])
+    landed(ext1.at[0, *mine], recv1x.at[0])
+    landed(ext1.at[1, *mine], recv1x.at[1])
     ey[0] = edges(both_sides(lambda side: ext1[side]))
     loads[3].wait()
 
@@ -298,9 +307,9 @@
     zero = jnp.zeros((8, 128), F32)
     moments = [levels(first_residual, zero)]
 
+    send_packed(2)
     remote(q_b.at[lev1, pl.ds(2, ROWS)], wide.at[2, 0, lev, pl.ds(2, ROWS)], send2.at[2, 0], recv2.at[2, 0], east)
     remote(q_b.at[lev1, pl.ds(2, ROWS)], wide.at[2, 1, lev, pl.ds(2, ROWS)], send2.at[2, 1], recv2.at[2, 1], west)
-    send_packed(2)
 
     def wait_ring(slot):
         east_rows, west_rows = (pl.ds(3, 3), pl.ds(2, 3)) if slot < 2 else (pl.ds(2, ROWS),) * 2
@@ -308,7 +317,7 @@
         landed(wide.at[slot, 1, lev, west_rows], recv2.at[slot, 1])
         for side in range(2):
             for j in range(3):
-                landed(ext2.at[slot, side, j], recv2x.at[slot, side, j])
+                landed(ext2.at[slot, side, j, *ring_rows(slot, j)], recv2x.at[slot, side, j])
 
     def gather(slot, ref, at, center, outer, center_at, plus):
         def step(p, _):
@@ -528,7 +537,7 @@
     return pl.pallas_call(
         kernel,
         out_shape=(block, block),
-        in_specs=[pl.BlockSpec(memory_space=pl.ANY)] * 4 + [pl.BlockSpec(memory_space=pltpu.SMEM)],
+        in_specs=[pl.BlockSpec(memory_space=pl.ANY)] * 5,
         out_specs=(pl.BlockSpec(memory_space=pl.ANY),) * 2,
         scratch_shapes=[
             *[field] * 8,
@@ -545,10 +554,11 @@
             pltpu.VMEM((SIZE_B, 128), F32),
             pltpu.VMEM((8, 128), F32),
             pltpu.VMEM((8, 128), F32),
+            pltpu.SMEM((LEV - 1,), F32),
             pltpu.SMEM((PAD + 2,), F32),
             field,
             field,
-            dma((4,)),
+            dma((5,)),
             dma((2,)),
             dma((2,)),
             dma((2,)),
@@ -559,7 +569,7 @@
             dma((3, 2, 3)),
             *[dma((1,))] * 4,
         ],
-        compiler_params=pltpu.CompilerParams(collective_id=0, has_side_effects=True, vmem_limit_bytes=48 << 20),
+        compiler_params=pltpu.CompilerParams(collective_id=0, has_side_effects=True, vmem_limit_bytes=60 << 20),
         cost_estimate=pl.CostEstimate(flops=8_000_000, bytes_accessed=900_000, transcendentals=0),
     )(right_side, first_guess, cell_scale, helmholtz_term, vertical_coupling)
 

time: 75.8 us -> 66.8 us (0.88)
  Pallas kernels: 69.4 us -> 63.7 us
  local copies, waits for them, and re-layouts: 5.6 us -> 2.28 us
    pallas_call x1, Pallas kernels: 69.4 us -> 63.7 us  [body(): pl.pallas_call(kernel, out_shape=(block, block), in_specs=[pl.BlockSpec(m...]
    unnamed x12 -> x4, local copies, waits for them, and re-layouts: 5.6 us -> 2.28 us
where the time goes in v2:
time: 66.8 us; the launch traced here: 66.6 us
  Pallas kernels  63.7 us (95%)
  local copies, waits for them, and re-layouts  2.28 us (3%)
    pallas_call x1, Pallas kernels, body(): pl.pallas_call(kernel, out_shape=(block, block), in_specs=[pl.BlockSpec(m...  63.7 us
    unnamed x4, local copies, waits for them, and re-layouts  2.28 us

profile of v2, /device:TPU:1, one launch (start us, length us, event | category | flops | bytes accessed | tf_op | source)
XLA Modules:
  0.0 66.6 jit_solution(1439418494649546618)
XLA Ops:
  0.6 63.7 %shard_map.68 = (f32[70,4,128]{2,1,0:T(4,128)}, f32[70,4,128]{2,1,0:T(4,128)}) custom-call(f32[70,4,128]{2,1,0:T(4,128)} %b_hbm.1, f32[70,4,128]{2,1,0:T(4,128)} %x_hbm.1, f32[70,4,128]{2,1,0:T(4,128)} %d_hbm.1, f32[70,4,128]{2,1,0:T(4,128)} %h_hbm.1, f32[69]{0:T(128)} %vc_hbm.1), custom_call_target="tpu_custom_call" | custom-call | flops 8000000 | bytes 900000 | tf_op jit(solution)/shard_map/pallas_call | solution.py:537
  64.3 0.0 copy-start
  64.3 1.6 %copy.9 = f32[70,4,128]{2,1,0:T(4,128)} copy(f32[70,4,128]{2,1,0:T(4,128)} %get-tuple-element.4) | data formatting | bytes 286720
  66.0 0.0 copy-done
  66.0 0.7 copy.10
Async XLA Ops:
  64.3 1.6 %copy-start = (f32[70,4,128]{2,1,0:T(4,128)S(1)}, f32[70,4,128]{2,1,0:T(4,128)}, u32[]{:S(2)}) copy-start(f32[70,4,128]{2,1,0:T(4,128)} %get-tuple-element.5) | copy-start | bytes 430084

commit v3 on v2

--- a/solution.py
+++ b/solution.py
@@ -93,40 +93,56 @@
     core, y_lo = lax.rem(band, NC), band // NC
     me_a = (y_hi * NYL + y_lo) * NX + x
     me_b = z * NC + core
-    group_a, group_b = [], []
-    for j in range(1, SIZE_A):
+
+    def peer_a(j):
         t = lax.rem(me_a + j, SIZE_A)
         px, py = lax.rem(t, NX), t // NX
-        group_a.append(((z * NYH + py // NYL) * NX + px, lax.rem(py, NYL) * NC + core))
-    for j in range(1, SIZE_B):
+        return (z * NYH + py // NYL) * NX + px, lax.rem(py, NYL) * NC + core
+
+    def peer_b(j):
         t = lax.rem(me_b + j, SIZE_B)
         pc, pz = lax.rem(t, NC), t // NC
-        group_b.append(((pz * NYH + y_hi) * NX + x, y_lo * NC + pc))
-    return (me_a, group_a), (me_b, group_b)
+        return (pz * NYH + y_hi) * NX + x, y_lo * NC + pc
+
+    return (me_a, peer_a), (me_b, peer_b)
+
+
+def repeat(start, stop, step):
+    def one(j, carry):
+        step(j)
+        return carry
+
+    lax.fori_loop(start, stop, one, 0)
 
 
 def kernel(
-    b_hbm, x_hbm, d_hbm, h_hbm, vc_hbm, sol_hbm, res_hbm,
-    b_in, x_in, d_in, h_in, d_c, h_c, d_o, h_o,
-    q_a, q_b, q_c, q_d, o_a, o_b,
-    near, wide, vs, packed, ext1, ext2, ex, ey, sums_a, sums_b, row_a, row_b, vc, couple, sol, res,
+    b_hbm, x_hbm, d_hbm, h_hbm, vc_hbm, sol_ref, res_ref,
+    b_in, x_in, dh, dh_c, dh_o, q_a, q_b, q_n, o_n,
+    near, wide, vs, packed, ext1, ext2, ex, ey, ring, moments, sums_a, sums_b, row_a, row_b, vc, couple,
     load_sem, send1, recv1, send1x, recv1x, send2, recv2, send2x, recv2x, send_a, recv_a, send_b, recv_b,
 ):
     beside, left, right, first, last = halo_peers()
-    (me_a, group_a), (me_b, group_b) = sum_peers()
+    (me_a, peer_a), (me_b, peer_b) = sum_peers()
 
     loads = [
         pltpu.make_async_copy(src, dst.at[pl.ds(0, LEV), pl.ds(2, ROWS)], load_sem.at[i])
-        for i, (src, dst) in enumerate(((d_hbm, d_in), (x_hbm, x_in), (h_hbm, h_in), (b_hbm, b_in)))
+        for i, (src, dst) in enumerate(((d_hbm, dh.at[0]), (x_hbm, x_in), (h_hbm, dh.at[1]), (b_hbm, b_in)))
     ]
     loads.append(pltpu.make_async_copy(vc_hbm, vc, load_sem.at[4]))
     for copy in loads:
         copy.start()
 
     barrier = pltpu.get_barrier_semaphore()
-    peers = [*beside, *left, *right, *group_a, *group_b]
-    for peer in peers:
+
+    def greet(peer):
         pl.semaphore_signal(barrier, inc=1, device_id=peer, device_id_type=MESH)
+
+    for peer in (*beside, *left, *right):
+        greet(peer)
+    for j in range(1, SIZE_B):
+        greet(peer_b(j))
+    for j in range(1, SIZE_A):
+        greet(peer_a(j))
 
     lane = lax.broadcasted_iota(jnp.int32, (8, 128), 1)
     sub = lax.broadcasted_iota(jnp.int32, (8, 128), 0)
@@ -137,12 +153,12 @@
     is_own = (sub >= 2) & (sub < 6)
 
     tail = jnp.zeros((PAD - LEV, 8, 128), F32)
-    for ref in (b_in, x_in, d_in, h_in, near):
+    for ref in (b_in, x_in, near, dh.at[0], dh.at[1]):
         ref[LEV:PAD] = tail
     for i in range(3):
         for j in range(2):
             wide[i, j, LEV:PAD] = tail
-    for ref in (q_a, q_b, q_c, q_d, o_a, o_b):
+    for ref in (q_a, q_b, q_n.at[0], q_n.at[1], o_n.at[0], o_n.at[1]):
         ref[0] = jnp.zeros((8, 128), F32)
         ref[PAD + 1] = jnp.zeros((8, 128), F32)
 
@@ -155,16 +171,6 @@
     def pack_in(tile, value, i):
         return jnp.where(lane8 == i, roll(value, 8 * i + 4, 1), tile)
 
-    def pack_field(ref, slot, at):
-        def step(p, _):
-            tile = jnp.zeros((8, 128), F32)
-            for i in range(GROUP):
-                tile = pack_in(tile, ref[p * GROUP + i + at], i)
-            packed[slot, p] = tile
-            return 0
-
-        levels(step, 0)
-
     loads[0].wait()
     loads[1].wait()
 
@@ -172,7 +178,7 @@
         tile = jnp.zeros((8, 128), F32)
         for i in range(GROUP):
             k = p * GROUP + i
-            value = d_in[k] * x_in[k]
+            value = dh[0, k] * x_in[k]
             q_a[k + 1] = value
             tile = pack_in(tile, value, i)
         packed[0, p] = tile
@@ -191,7 +197,7 @@
         pltpu.make_async_copy(ref, ref, sem).wait()
 
     sends = []
-    pl.semaphore_wait(barrier, len(peers))
+    pl.semaphore_wait(barrier, 8 + SIZE_A - 1 + SIZE_B - 1)
 
     lev = pl.ds(0, LEV)
     lev1 = pl.ds(1, LEV)
@@ -217,18 +223,36 @@
                    recv2x.at[slot, right_side, at], right[j])
 
     loads[2].wait()
-    for slot, ref in ((0, d_in), (1, h_in)):
-        remote(ref.at[lev, pl.ds(3, 3)], wide.at[slot, 0, lev, pl.ds(3, 3)], send2.at[slot, 0], recv2.at[slot, 0], east)
-        remote(ref.at[lev, pl.ds(2, 3)], wide.at[slot, 1, lev, pl.ds(2, 3)], send2.at[slot, 1], recv2.at[slot, 1], west)
-    for slot, ref in ((0, d_in), (1, h_in)):
-        pack_field(ref, slot + 1, 0)
+    for slot in range(2):
+        remote(dh.at[slot, lev, pl.ds(3, 3)], wide.at[slot, 0, lev, pl.ds(3, 3)], send2.at[slot, 0],
+               recv2.at[slot, 0], east)
+        remote(dh.at[slot, lev, pl.ds(2, 3)], wide.at[slot, 1, lev, pl.ds(2, 3)], send2.at[slot, 1],
+               recv2.at[slot, 1], west)
+
+    def pack_coefficients(s):
+        slot, p = s // GROUPS, lax.rem(s, GROUPS)
+        tile = jnp.zeros((8, 128), F32)
+        for i in range(GROUP):
+            tile = pack_in(tile, dh[slot, p * GROUP + i], i)
+        packed[slot + 1, p] = tile
+
+    repeat(0, 2 * GROUPS, pack_coefficients)
+    for slot in range(2):
         send_packed(slot)
 
     loads[4].wait()
-    for k in range(PAD + 2):
-        couple[k] = vc[k - 1] if 1 <= k < LEV else jnp.float32(0.0)
-
-    for p in range(GROUPS):
+    couple[0] = jnp.float32(0.0)
+
+    def couple_in(k):
+        couple[k] = vc[k - 1]
+
+    def couple_none(k):
+        couple[k] = jnp.float32(0.0)
+
+    repeat(1, LEV, couple_in)
+    repeat(LEV, PAD + 2, couple_none)
+
+    def couple_tiles(p):
         below = jnp.zeros((8, 128), F32)
         above = jnp.zeros((8, 128), F32)
         for i in range(GROUP):
@@ -238,6 +262,8 @@
             above = jnp.where(here, couple[k], above)
         ey[1, p] = below
         ey[2, p] = above
+
+    repeat(0, GROUPS, couple_tiles)
 
     def mirrored(value, side):
         if side == 0:
@@ -274,9 +300,8 @@
         e = roll(edge, 124 - 8 * i, 1)
         return jnp.where(lane == 0, e, roll(q, 1, 1)) + jnp.where(lane == 127, e, roll(q, -1, 1))
 
-    def stencil(q, up, down, h4, lon_sum, lat, k):
-        flux = couple[k + 1] * (q - down) - couple[k] * (up - q)
-        return h4 * q - lon_sum - lat + flux
+    def stencil(q, below, above, h4, lon_sum, lat):
+        return h4 * q - lon_sum - lat + (below - above)
 
     landed(near.at[lev, pl.ds(5, 1)], recv1.at[0])
     landed(near.at[lev, pl.ds(2, 1)], recv1.at[1])
@@ -286,6 +311,7 @@
     loads[3].wait()
 
     def first_residual(p, acc):
+        acc, above = acc
         tile = jnp.zeros((8, 128), F32)
         edge = ey[0, p]
         for i in range(GROUP):
@@ -293,8 +319,10 @@
             q = q_a[k + 1]
             n = roll(near[k], 4, 0)
             lon_sum = roll(jnp.where(sub == 6, n, q), -1, 0) + roll(jnp.where(sub == 1, n, q), 1, 0)
-            d = d_in[k]
-            t = stencil(q, q_a[k], q_a[k + 2], 4.0 + h_in[k], lon_sum, lat_sum(q, edge, i), k)
+            d = dh[0, k]
+            below = couple[k + 1] * (q - q_a[k + 2])
+            t = stencil(q, below, above, 4.0 + dh[1, k], lon_sum, lat_sum(q, edge, i))
+            above = below
             r = b_in[k] - d * t
             vs[0, k] = r
             acc = acc + r * r
@@ -302,10 +330,10 @@
             q_b[k + 1] = value
             tile = pack_in(tile, value, i)
         packed[3, p] = tile
-        return acc
+        return acc, above
 
     zero = jnp.zeros((8, 128), F32)
-    moments = [levels(first_residual, zero)]
+    moments[0], _ = levels(first_residual, (zero, zero))
 
     send_packed(2)
     remote(q_b.at[lev1, pl.ds(2, ROWS)], wide.at[2, 0, lev, pl.ds(2, ROWS)], send2.at[2, 0], recv2.at[2, 0], east)
@@ -319,33 +347,46 @@
             for j in range(3):
                 landed(ext2.at[slot, side, j, *ring_rows(slot, j)], recv2x.at[slot, side, j])
 
-    def gather(slot, ref, at, center, outer, center_at, plus):
-        def step(p, _):
-            for i in range(GROUP):
-                k = p * GROUP + i
-                w, e = roll(wide[slot, 0, k], 4, 0), roll(wide[slot, 1, k], 4, 0)
-                mine = ref[k + at]
-                center[k + center_at] = jnp.where(sub < 2, w, jnp.where(sub >= 6, e, mine)) + plus
-                outer[k + center_at] = jnp.where(sub < 2, e, w) + plus
-            return 0
-
-        levels(step, 0)
-
-    for slot, ref, center, outer, plus in ((0, d_in, d_c, d_o, 0.0), (1, h_in, h_c, h_o, 4.0)):
-        wait_ring(slot)
-        gather(slot, ref, 0, center, outer, 0, plus)
-        ex[slot] = ring_center(slot) + plus
+    def ring_and_mine(slot, k, mine):
+        w, e = roll(wide[slot, 0, k], 4, 0), roll(wide[slot, 1, k], 4, 0)
+        return jnp.where(sub < 2, w, jnp.where(sub >= 6, e, mine)), jnp.where(sub < 2, e, w)
+
+    def gather_coefficients(s):
+        slot, p = s // (PAD // 8), lax.rem(s, PAD // 8)
+        plus = 4.0 * slot.astype(F32)
+        for i in range(8):
+            k = p * 8 + i
+            center, outer = ring_and_mine(slot, k, dh[slot, k])
+            dh_c[slot, k] = center + plus
+            dh_o[slot, k] = outer + plus
+
+    def gather_field(p):
+        tile = jnp.zeros((8, 128), F32)
+        for i in range(GROUP):
+            k = p * GROUP + i
+            center, outer = ring_and_mine(2, k, q_b[k + 1])
+            q_n[0, k + 1] = center
+            o_n[0, k + 1] = outer
+            tile = pack_in(tile, center, i)
+        ex[2, p] = tile
+
+    wait_ring(0)
+    wait_ring(1)
+    repeat(0, 2 * (PAD // 8), gather_coefficients)
+    ex[0] = ring_center(0)
+    ex[1] = ring_center(1) + 4.0
     wait_ring(2)
-    gather(2, q_b, 1, q_c, o_a, 1, 0.0)
-    ring = ring_center(2)
+    repeat(0, GROUPS, gather_field)
+    ring[...] = ring_center(2)
     ring_o = ring_outer(2)
-    ey[0] = edges(ring)
+    ey[0] = edges(ring[...])
     ey[3] = edges(ring_o)
+    ex[4] = ring_o
 
     def ring_step(x, edge_tiles, outer):
         right_of = roll(jnp.where(col5 == 4, edge_tiles, x), -1, 2)
         left_of = roll(jnp.where(col5 == 3, edge_tiles, x), 1, 2)
-        o = x if outer is None else outer
+        o = outer
         lon_sum = roll(jnp.where(sub5 == 0, o, x), -1, 1) + roll(jnp.where(sub5 == 7, o, x), 1, 1)
         ahead, behind = roll(x, -8, 2), roll(x, 8, 2)
         none = jnp.zeros((1, 8, 128), F32)
@@ -355,66 +396,75 @@
         d = ex[0]
         return d * (d * t)
 
-    def apply(n, src, dst, out_src, out_dst, slot):
+    def outer_step(p):
+        out = []
+        edge = ey[3, p]
+        above = couple[p * GROUP] * (o_n[0, p * GROUP] - o_n[0, p * GROUP + 1])
+        for i in range(GROUP):
+            k = p * GROUP + i
+            o, q = o_n[0, k + 1], q_n[0, k + 1]
+            lon_sum = roll(jnp.where(sub == 0, q, o), -1, 0) + roll(jnp.where(sub == 7, q, o), 1, 0)
+            d = dh_o[0, k]
+            below = couple[k + 1] * (o - o_n[0, k + 2])
+            t = stencil(o, below, above, dh_o[1, k], lon_sum, lat_sum(o, edge, i))
+            above = below
+            out.append(d * (d * t))
+        for i in range(GROUP):
+            o_n[1, p * GROUP + i + 1] = out[i]
+
+    repeat(0, GROUPS, outer_step)
+
+    def packed_group(slot, p):
+        tile = jnp.zeros((8, 128), F32)
+        for i in range(GROUP):
+            tile = pack_in(tile, q_n[slot, p * GROUP + i + 1], i)
+        return tile
+
+    def apply(n):
+        src, dst = lax.rem(n + 1, 2), lax.rem(n, 2)
+        beyond = jnp.minimum(n - 1, 1)
+
         def step(p, acc):
-            even, odd = acc
-            tile = jnp.zeros((8, 128), F32)
+            even, odd, above = acc
             edge = ey[0, p]
-            edge_o = ey[3, p]
+            out = []
+            before = jnp.maximum(p - 1, 0)
+            ex[2 + dst, before] = packed_group(dst, before)
             for i in range(GROUP):
                 k = p * GROUP + i
-                q = src[k + 1]
-                o = q if out_src is None else out_src[k + 1]
+                q, o = q_n[src, k + 1], o_n[beyond, k + 1]
                 lon_sum = roll(jnp.where(sub == 0, o, q), -1, 0) + roll(jnp.where(sub == 7, o, q), 1, 0)
-                d = d_c[k]
-                v = d * stencil(q, src[k], src[k + 2], h_c[k], lon_sum, lat_sum(q, edge, i), k)
-                vs[n, k] = v
+                d = dh_c[0, k]
+                below = couple[k + 1] * (q - q_n[src, k + 2])
+                v = d * stencil(q, below, above, dh_c[1, k], lon_sum, lat_sum(q, edge, i))
+                above = below
                 odd = odd + vs[n - 1, k] * v
                 even = even + v * v
-                if dst is not None:
-                    value = d * v
-                    dst[k + 1] = value
-                    tile = pack_in(tile, value, i)
-                if out_dst is not None:
-                    lon_o = roll(jnp.where(sub == 0, q, o), -1, 0) + roll(jnp.where(sub == 7, q, o), 1, 0)
-                    do = d_o[k]
-                    to = stencil(o, out_src[k], out_src[k + 2], h_o[k], lon_o, lat_sum(o, edge_o, i), k)
-                    out_dst[k + 1] = do * (do * to)
-            if dst is not None:
-                ex[slot, p] = tile
-            return even, odd
-
-        even, odd = levels(step, (zero, zero))
-        moments.extend([odd, even])
-
-    def pack_ref(ref, slot):
-        def step(p, _):
-            tile = jnp.zeros((8, 128), F32)
+                out.append((v, d * v))
             for i in range(GROUP):
-                tile = pack_in(tile, ref[p * GROUP + i + 1], i)
-            ex[slot, p] = tile
-            return 0
-
-        levels(step, 0)
-
-    pack_ref(q_c, 2)
-    apply(1, q_c, q_d, o_a, o_b, 3)
-    ring = ring_step(ring, ex[2], ring_o)
-    ey[0] = edges(ring)
-    apply(2, q_d, q_c, o_b, None, 2)
-    ring = ring_step(ring, ex[3], None)
-    ey[0] = edges(ring)
-    apply(3, q_c, q_d, None, None, 3)
-    ring = ring_step(ring, ex[2], None)
-    ey[0] = edges(ring)
-    apply(4, q_d, None, None, None, 2)
+                k = p * GROUP + i
+                vs[n, k], q_n[dst, k + 1] = out[i]
+            return even, odd, above
+
+        even, odd, _ = levels(step, (zero, zero, zero))
+        ex[2 + dst, GROUPS - 1] = packed_group(dst, GROUPS - 1)
+        moments[2 * n - 1] = odd
+        moments[2 * n] = even
+
+        @pl.when(n < 4)
+        def _():
+            value = ring_step(ring[...], ex[2 + src], ex[4])
+            ring[...] = value
+            ey[0] = edges(value)
+
+    repeat(1, 5, apply)
 
     def total(acc):
         value = jnp.where(is_own, acc, 0.0)
         pair = two_sum(value, roll(value, -2, 0))
         return dd_add(pair, tuple(roll(part, -1, 0) for part in pair))
 
-    pairs = [total(acc) for acc in moments]
+    pairs = [total(moments[k]) for k in range(9)]
     row = jnp.zeros((8, 128), F32)
     for start in (0, 8):
         high, low = zero, zero
@@ -429,15 +479,19 @@
     for width in (4, 2, 1):
         row = row + roll(row, width, 0)
 
-    def sum_over(row, line, slots, me, group, size, send, recv):
+    def sum_over(row, line, slots, me, peer, size, send, recv):
         line[...] = row
         slots[pl.ds(me, 1), :] = row[0:1]
-        for peer in group:
+
+        def give(j):
             copy = pltpu.make_async_remote_copy(
                 src_ref=line.at[pl.ds(0, 1)], dst_ref=slots.at[pl.ds(me, 1)], send_sem=send.at[0],
-                recv_sem=recv.at[0], device_id=peer, device_id_type=MESH,
+                recv_sem=recv.at[0], device_id=peer(j), device_id_type=MESH,
             )
             copy.start()
+
+        for j in range(1, size):
+            give(j)
         landed(slots.at[pl.ds(0, size - 1)], recv.at[0])
         parts = [(slots[8 * j : 8 * j + 8], zero) for j in range(size // 8)]
         while len(parts) > 1:
@@ -455,8 +509,8 @@
         s, e = two_sum(a[0], b[0])
         return s, e + (a[1] + b[1])
 
-    row = sum_over(row, row_a, sums_a, me_a, group_a, SIZE_A, send_a, recv_a)
-    row = sum_over(row, row_b, sums_b, me_b, group_b, SIZE_B, send_b, recv_b)
+    row = sum_over(row, row_a, sums_a, me_a, peer_a, SIZE_A, send_a, recv_a)
+    row = sum_over(row, row_b, sums_b, me_b, peer_b, SIZE_B, send_b, recv_b)
 
     m = (row, roll(row, -16, 1))
 
@@ -506,27 +560,20 @@
         dd_mul(omega1, h3),
     )
 
-    def finish(p, _):
-        for i in range(GROUP):
-            k = p * GROUP + i
+    def finish(p):
+        for i in range(7):
+            k = p * 7 + i
             v = [vs[n, k] for n in range(5)]
-            sol[k] = x_in[k] + (sol_c[0][0] * v[0] + sol_c[1][0] * v[1] + sol_c[2][0] * v[2] + sol_c[3][0] * v[3])
-            res[k] = v[0] + (res_c[1][0] * v[1] + res_c[2][0] * v[2] + res_c[3][0] * v[3] + res_c[4][0] * v[4])
-        return 0
-
-    levels(finish, 0)
-    stores = [
-        pltpu.make_async_copy(src.at[lev, pl.ds(2, ROWS)], dst, load_sem.at[i])
-        for i, (src, dst) in enumerate(((sol, sol_hbm), (res, res_hbm)))
-    ]
-    for copy in stores:
-        copy.start()
+            moved = sol_c[0][0] * v[0] + sol_c[1][0] * v[1] + sol_c[2][0] * v[2] + sol_c[3][0] * v[3]
+            left_over = res_c[1][0] * v[1] + res_c[2][0] * v[2] + res_c[3][0] * v[3] + res_c[4][0] * v[4]
+            sol_ref[k] = (x_in[k] + moved)[2:6]
+            res_ref[k] = (v[0] + left_over)[2:6]
+
+    repeat(0, LEV // 7, finish)
     for copy in sends:
         copy.wait_send()
     landed(sums_a.at[pl.ds(0, SIZE_A - 1)], send_a.at[0])
     landed(sums_b.at[pl.ds(0, SIZE_B - 1)], send_b.at[0])
-    for copy in stores:
-        copy.wait()
 
 
 def body(right_side, first_guess, cell_scale, helmholtz_term, vertical_coupling):
@@ -537,27 +584,31 @@
     return pl.pallas_call(
         kernel,
         out_shape=(block, block),
-        in_specs=[pl.BlockSpec(memory_space=pl.ANY)] * 5,
-        out_specs=(pl.BlockSpec(memory_space=pl.ANY),) * 2,
+        in_specs=[pl.BlockSpec(memory_space=pltpu.HBM)] * 5,
+        out_specs=(pl.BlockSpec(memory_space=pltpu.VMEM),) * 2,
         scratch_shapes=[
-            *[field] * 8,
-            *[guarded] * 6,
+            field,
+            field,
+            *[pltpu.VMEM((2, PAD, 8, 128), F32)] * 3,
+            guarded,
+            guarded,
+            *[pltpu.VMEM((2, PAD + 2, 8, 128), F32)] * 2,
             field,
             pltpu.VMEM((3, 2, PAD, 8, 128), F32),
             pltpu.VMEM((5, PAD, 8, 128), F32),
             pltpu.VMEM((4, GROUPS, 8, 128), F32),
             pltpu.VMEM((2, GROUPS, 8, 128), F32),
             pltpu.VMEM((3, 2, 3, GROUPS, 8, 128), F32),
+            pltpu.VMEM((5, GROUPS, 8, 128), F32),
             pltpu.VMEM((4, GROUPS, 8, 128), F32),
-            pltpu.VMEM((4, GROUPS, 8, 128), F32),
+            pltpu.VMEM((GROUPS, 8, 128), F32),
+            pltpu.VMEM((9, 8, 128), F32),
             pltpu.VMEM((SIZE_A, 128), F32),
             pltpu.VMEM((SIZE_B, 128), F32),
             pltpu.VMEM((8, 128), F32),
             pltpu.VMEM((8, 128), F32),
             pltpu.SMEM((LEV - 1,), F32),
             pltpu.SMEM((PAD + 2,), F32),
-            field,
-            field,
             dma((5,)),
             dma((2,)),
             dma((2,)),
@@ -569,7 +620,7 @@
             dma((3, 2, 3)),
             *[dma((1,))] * 4,
         ],
-        compiler_params=pltpu.CompilerParams(collective_id=0, has_side_effects=True, vmem_limit_bytes=60 << 20),
+        compiler_params=pltpu.CompilerParams(collective_id=0, has_side_effects=True, vmem_limit_bytes=54920 << 10),
         cost_estimate=pl.CostEstimate(flops=8_000_000, bytes_accessed=900_000, transcendentals=0),
     )(right_side, first_guess, cell_scale, helmholtz_term, vertical_coupling)
 

time: 66.8 us -> 65.6 us (0.982)
  Pallas kernels: 63.7 us -> 62.9 us
    pallas_call x1, Pallas kernels: 63.7 us -> 62.9 us  [body(): pl.pallas_call(kernel, out_shape=(block, block), in_specs=[pl.BlockSpec(m...]
where the time goes in v3:
time: 65.6 us; the launch traced here: 65.5 us
  Pallas kernels  62.9 us (96%)
  local copies, waits for them, and re-layouts  1.97 us (3%)
    pallas_call x1, Pallas kernels, body(): pl.pallas_call(kernel, out_shape=(block, block), in_specs=[pl.BlockSpec(m...  62.9 us
    unnamed x4, local copies, waits for them, and re-layouts  1.97 us

profile of v3, /device:TPU:1, one launch (start us, length us, event | category | flops | bytes accessed | tf_op | source)
XLA Modules:
  0.0 65.5 jit_solution(14227435749931900457)
XLA Ops:
  0.6 0.0 copy-start
  0.6 0.6 copy-done
  1.3 62.9 %shard_map.68 = (f32[70,4,128]{2,1,0:T(4,128)S(1)}, f32[70,4,128]{2,1,0:T(4,128)S(1)}) custom-call(f32[70,4,128]{2,1,0:T(4,128)} %b_hbm.1, f32[70,4,128]{2,1,0:T(4,128)} %x_hbm.1, f32[70,4,128]{2,1,0:T(4,128)} %d_hbm.1, f32[70,4,128]{2,1,0:T(4,128)} %h_hbm.1, f32[69]{0:T(128)S(1)} %copy-done), custom_call_target="tpu_custom_call" | custom-call | flops 8000000 | bytes 900000 | tf_op jit(solution)/shard_map/pallas_call | solution.py:584
  64.2 0.7 %copy.9 = f32[70,4,128]{2,1,0:T(4,128)} copy(f32[70,4,128]{2,1,0:T(4,128)S(1)} %get-tuple-element.4) | data formatting | bytes 286720
  64.8 0.7 %copy.10 = f32[70,4,128]{2,1,0:T(4,128)} copy(f32[70,4,128]{2,1,0:T(4,128)S(1)} %get-tuple-element.5) | data formatting | bytes 286720
Async XLA Ops:
  0.6 0.7 %copy-start = (f32[69]{0:T(128)S(1)}, f32[69]{0:T(128)}, u32[]{:S(2)}) copy-start(f32[69]{0:T(128)} %vc_hbm.1) | copy-start | bytes 832

commit v4 on v3

--- a/solution.py
+++ b/solution.py
@@ -446,7 +446,7 @@
                 vs[n, k], q_n[dst, k + 1] = out[i]
             return even, odd, above
 
-        even, odd, _ = levels(step, (zero, zero, zero))
+        even, odd, _ = lax.fori_loop(0, GROUPS, step, (zero, zero, zero), unroll=GROUPS)
         ex[2 + dst, GROUPS - 1] = packed_group(dst, GROUPS - 1)
         moments[2 * n - 1] = odd
         moments[2 * n] = even

time: 65.6 us -> 65.1 us (level)
  no operation moved by 1% of the time
where the time goes in v4:
time: 65.1 us; the launch traced here: 65 us
  Pallas kernels  62.4 us (96%)
  local copies, waits for them, and re-layouts  1.97 us (3%)
    pallas_call x1, Pallas kernels, body(): pl.pallas_call(kernel, out_shape=(block, block), in_specs=[pl.BlockSpec(m...  62.4 us
    unnamed x4, local copies, waits for them, and re-layouts  1.97 us

profile of v4, /device:TPU:1, one launch (start us, length us, event | category | flops | bytes accessed | tf_op | source)
XLA Modules:
  0.0 65.0 jit_solution(4904852754379187866)
XLA Ops:
  0.6 0.0 copy-start
  0.6 0.6 copy-done
  1.3 62.4 %shard_map.68 = (f32[70,4,128]{2,1,0:T(4,128)S(1)}, f32[70,4,128]{2,1,0:T(4,128)S(1)}) custom-call(f32[70,4,128]{2,1,0:T(4,128)} %b_hbm.1, f32[70,4,128]{2,1,0:T(4,128)} %x_hbm.1, f32[70,4,128]{2,1,0:T(4,128)} %d_hbm.1, f32[70,4,128]{2,1,0:T(4,128)} %h_hbm.1, f32[69]{0:T(128)S(1)} %copy-done), custom_call_target="tpu_custom_call" | custom-call | flops 8000000 | bytes 900000 | tf_op jit(solution)/shard_map/pallas_call | solution.py:584
  63.7 0.7 %copy.9 = f32[70,4,128]{2,1,0:T(4,128)} copy(f32[70,4,128]{2,1,0:T(4,128)S(1)} %get-tuple-element.4) | data formatting | bytes 286720
  64.3 0.7 %copy.10 = f32[70,4,128]{2,1,0:T(4,128)} copy(f32[70,4,128]{2,1,0:T(4,128)S(1)} %get-tuple-element.5) | data formatting | bytes 286720
Async XLA Ops:
  0.6 0.7 %copy-start = (f32[69]{0:T(128)S(1)}, f32[69]{0:T(128)}, u32[]{:S(2)}) copy-start(f32[69]{0:T(128)} %vc_hbm.1) | copy-start | bytes 832
